TPU v7x, 512 devices: a whole 4x4x16 slice. The times are simulated.
512 devices in a mesh: member: 8 (over y, core), dp: 32 (over z, x_lo), tensor: 2 (over x_hi).
Axes of the slice: x: 4 (x_hi: 2, x_lo: 2; x = x_hi * 2 + x_lo), y: 4, z: 16, core: 2. Of those that a mesh axis runs over, the one named last changes fastest.
Arguments:
- context: bfloat16 [8, 32, 128, 2560], P('member', 'dp', None, 'tensor')
- out_weight: bfloat16 [8, 5120, 2560], P('member', 'dp', 'tensor')
- first_moment: float32 [8, 5120, 2560], P('member', 'dp', 'tensor'), may hold values from -0.75 to 0.75
- second_moment: float32 [8, 5120, 2560], P('member', 'dp', 'tensor'), may hold values from 0.001 to 0.01
- target: bfloat16 [8, 32, 128, 5120], P('member', None, 'tensor', 'dp'), may hold values from -6 to 6
- token_ids: int32 [8, 32, 128], P('member'), may hold values from 0 to 31999, as said below
- base_lr: float32 [8], replicated, may hold values from 0.02 to 0.2
- perturb_index: int32 [8], replicated, may hold values from 0 to 8
- partner: int32 [8, 32], P(None, 'dp'), may hold values from 0 to 7, as said below
Outputs:
- new_weight: bfloat16 [8, 5120, 2560], P('member', 'dp', 'tensor')
- new_first: float32 [8, 5120, 2560], P('member', 'dp', 'tensor')
- new_second: float32 [8, 5120, 2560], P('member', 'dp', 'tensor')
Inputs may be any that keep to these rules, and one draw needn't show every extreme that they name: `token_ids`: 0 marks padding; in each window of 128 tokens the padding, if any, is the final run and covers at most half of the window; the largest id occurs. `partner`: in each slab s, every member names itself except the losers of that slab; each loser names a different member, and a named member names itself.
All inputs are finite; a program needn't handle non-finite values.
Results may differ from a plain program's by a relative error of at most 0.0021.
Values may be sent and summed in bfloat16 or wider, within the bound.
A program may use at most 128 MiB of HBM per device.

v0:
```python
import math

import jax
import jax.numpy as jnp
from jax import lax
from jax.sharding import PartitionSpec as P

D = 5120
HW = 2560


beta_one = 0.9
beta_two = 0.95
norm_eps = 1e-05
adam_eps = 1e-08


def weight_gradient(outputs, goal, loss_mask, gathered):
    scaling = 1.0 / math.sqrt(HW)
    squares, cross_sums = lax.psum(
        (jnp.sum(outputs * outputs, axis=0), jnp.sum(goal * outputs, axis=0)), "dp"
    )
    inverse = lax.rsqrt(squares / D + norm_eps)
    projection = loss_mask * (inverse * inverse * squares - inverse * cross_sums) / D
    normed = outputs * inverse
    hidden_grad = loss_mask * (normed - goal)
    grad_out = (inverse * (hidden_grad - normed * projection)).astype(jnp.bfloat16)
    return jnp.dot(grad_out, gathered, preferred_element_type=jnp.float32) * scaling


def route_weights(values, partner_column):
    shaped = values.reshape((1,) + values.shape)
    spread = lax.all_to_all(shaped, "member", split_axis=2, concat_axis=0, tiled=True)
    picked = jnp.take(spread, partner_column, axis=0)
    return lax.all_to_all(picked, "member", split_axis=0, concat_axis=2, tiled=True)[0]


def route_moments(first_new, second_new, partner_column):
    first_shaped = first_new.reshape((1,) + first_new.shape)
    second_shaped = second_new.reshape((1,) + second_new.shape)
    first_spread, second_spread = (
        lax.all_to_all(first_shaped, "member", split_axis=2, concat_axis=0, tiled=True),
        lax.all_to_all(second_shaped, "member", split_axis=2, concat_axis=0, tiled=True),
    )
    first_picked = jnp.take(first_spread, partner_column, axis=0)
    second_picked = jnp.take(second_spread, partner_column, axis=0)
    first_back, second_back = (
        lax.all_to_all(first_picked, "member", split_axis=0, concat_axis=2, tiled=True),
        lax.all_to_all(second_picked, "member", split_axis=0, concat_axis=2, tiled=True),
    )
    return (first_back[0], second_back[0])


def body(
    context,
    out_weight,
    first_moment,
    second_moment,
    target,
    token_ids,
    base_lr,
    perturb_index,
    partner,
):
    scaling = 1.0 / math.sqrt(HW)
    local_rows = context[0, 0]
    weight_local = out_weight[0]
    goal_local = target[0]
    id_table = token_ids[0]
    partner_column = partner[:, 0]
    gathered = lax.all_gather(local_rows, "dp", axis=0, tiled=True)
    partial_out = (
        lax.dot_general(
            weight_local, gathered, (((1,), (1,)), ((), ())), preferred_element_type=jnp.float32
        )
        * scaling
    )
    outputs = lax.psum(partial_out, "tensor")
    goal_full = lax.all_gather(goal_local, "tensor", axis=1, tiled=True)
    goal = goal_full.reshape(-1, goal_full.shape[-1]).T.astype(jnp.float32)
    loss_mask = (id_table.reshape(-1) != 0).astype(jnp.float32)
    gradient = weight_gradient(outputs, goal, loss_mask, gathered)
    first_new = beta_one * first_moment[0] + (1.0 - beta_one) * gradient
    second_new = beta_two * second_moment[0] + (1.0 - beta_two) * gradient * gradient
    step_sizes = base_lr * 2.0 ** ((perturb_index.astype(jnp.float32) - 4.0) / 4.0)
    member_index = lax.axis_index("member")
    stepped = (
        weight_local.astype(jnp.float32)
        - step_sizes[member_index] * first_new / (jnp.sqrt(second_new) + adam_eps)
    ).astype(jnp.bfloat16)
    new_weight = route_weights(stepped, partner_column)
    new_first, new_second = route_moments(first_new, second_new, partner_column)
    return (new_weight[None], new_first[None], new_second[None])


def solution(mesh):
    return jax.shard_map(
        body,
        mesh=mesh,
        in_specs=(
            P("member", "dp", None, "tensor"),
            P("member", "dp", "tensor"),
            P("member", "dp", "tensor"),
            P("member", "dp", "tensor"),
            P("member", None, "tensor", "dp"),
            P("member", None, None),
            P(),
            P(),
            P(None, "dp"),
        ),
        out_specs=(
            P("member", "dp", "tensor"),
            P("member", "dp", "tensor"),
            P("member", "dp", "tensor"),
        ),
        check_vma=False,
    )
```

profile of v0, /device:TPU:1, one launch (start us, length us, event | category | flops | bytes accessed | tf_op | source)
XLA Modules:
  0.0 677.7 jit_solution(13405818387870988712)
XLA Ops:
  8.0 2.9 copy.71
  10.9 241.4 %all-gather.5.cloned.1.call-done = bf16[1,1,4096,1280]{3,2,1,0:T(8,128)(2,1)} async-done(((bf16[1,1,128,1280]{3,2,1,0:T(8,128)(2,1)}), bf16[1,1,4096,1280]{3,2,1,0:T(8,128)(2,1)}) %all-gather.5.cloned.1.call-update) | async-done | bytes 10485776 | tf_op jit(solution)/shard_map/all_gather | solution.py:71
  252.3 9.0 %fusion.4 = f32[160,4096]{1,0:T(8,128)} fusion(bf16[1,1,4096,1280]{3,2,1,0:T(8,128)(2,1)} %all-gather.5.cloned.1.call-done, bf16[1,160,1280]{2,1,0:T(8,128)(2,1)S(1)} %copy-done.2), kind=kOutput, calls=%fused_computation.7 | convolution fusion | flops 1678376960 | bytes 13516800 | tf_op jit(solution)/shard_map/dot_general | solution.py:73
  262.6 38.2 %all-gather.7.cloned.1.call-done = bf16[1,32,128,160]{3,1,0,2:T(8,128)(2,1)} async-done(((bf16[1,32,64,160]{3,1,0,2:T(8,128)(2,1)}), bf16[1,32,128,160]{3,1,0,2:T(8,128)(2,1)}) %all-gather.7.cloned.1.call-update) | async-done | bytes 1310736 | tf_op jit(solution)/shard_map/all_gather | solution.py:79
  300.7 4.4 copy.72
  306.8 94.2 %all-reduce.3.cloned.1.call-done = f32[160,4096]{1,0:T(8,128)} async-done(((f32[160,4096]{1,0:T(8,128)}), f32[160,4096]{1,0:T(8,128)}) %all-reduce.3.cloned.1.call-update) | async-done | bytes 2621456 | tf_op jit(solution)/shard_map/psum | solution.py:78
  401.0 3.4 multiply_reduce_fusion
  404.5 94.9 %all-reduce = (f32[4096]{0:T(1024)S(1)}, f32[4096]{0:T(1024)S(1)}) all-reduce(f32[4096]{0:T(1024)S(1)} %get-tuple-element.5, f32[4096]{0:T(1024)S(1)} %get-tuple-element.4), channel_id=1, replica_groups=mesh['member'=8,'dp'=32,'tensor'=2] {'dp'}, use_global_device_ids=true, to_apply=%region_4.0 | all-reduce | flops 8192 | bytes 65536 | tf_op jit(solution)/shard_map/psum | solution.py:20
  499.4 10.6 %fusion.21 = (f32[1,160,1280]{2,1,0:T(8,128)}, bf16[1,160,1280]{2,1,0:T(8,128)(2,1)S(1)}, f32[1,160,1280]{2,1,0:T(8,128)}) fusion(f32[1,160,1280]{2,1,0:T(8,128)} %param.14, f32[1,160,1280]{2,1,0:T(8,128)} %param.13, f32[]{:T(128)} %bitcast.2, bf16[1,160,1280]{2,1,0:T(8,128)(2,1)S(1)} %copy-done.2, ...), kind=kOutput, calls=%fused_computation.29 | convolution fusion | flops 1685176320 | bytes 19873796 | tf_op jit(solution)/shard_map/dot_general | solution.py:28
  512.4 7.5 %reduce = bf16[1280,160]{1,0:T(8,128)(2,1)S(1)} reduce(bf16[1280,1,160]{2,1,0:T(2,128)(2,1)S(1)} %bitcast.122, bf16[]{:T(256)} %broadcast.101), dimensions={1}, to_apply=%bitcast.108.reduce_sub_computation | reduce | bytes 819202
  521.7 32.6 %all-to-all-start = ((bf16[8,2,12800]{2,1,0:T(2,128)(2,1)}), bf16[8,2,12800]{2,1,0:T(2,128)(2,1)S(1)}, u32[]{:S(2)}, u32[]{:S(2)}) async-start(bf16[8,2,12800]{2,1,0:T(2,128)(2,1)} %reshape.82), calls=%async_computation | async-start | bytes 819200 | tf_op jit(solution)/shard_map/all_to_all | solution.py:33
  556.4 6.1 all-to-all-done
  562.5 4.3 all-to-all-start.2
  569.0 15.7 %all-to-all-done.2 = f32[1,160,1280]{1,0,2:T(1,128)S(1)} async-done(((f32[1,160,1280]{1,0,2:T(1,128)}), f32[1,160,1280]{1,0,2:T(1,128)S(1)}, u32[]{:S(2)}, u32[]{:S(2)}) %all-to-all-start.2) | async-done | bytes 819232 | tf_op jit(solution)/shard_map/all_to_all | solution.py:42
  584.7 4.3 all-to-all-start.4
  589.1 2.3 reshape.83
  596.6 10.4 %all-to-all-done.4 = f32[1,160,1280]{1,0,2:T(1,128)S(1)} async-done(((f32[1,160,1280]{1,0,2:T(1,128)}), f32[1,160,1280]{1,0,2:T(1,128)S(1)}, u32[]{:S(2)}, u32[]{:S(2)}) %all-to-all-start.4) | async-done | bytes 819232 | tf_op jit(solution)/shard_map/all_to_all | solution.py:43
  607.0 4.3 all-to-all-start.1
  620.9 3.1 broadcast_select_fusion
  624.0 22.5 %all_to_all.108 = f32[8,160,160]{2,1,0:T(8,128)S(1)} all-to-all(f32[8,160,160]{2,1,0:T(8,128)S(1)} %get-tuple-element.15), channel_id=1, replica_groups=mesh['member'=8,'dp'=32,'tensor'=2] {'member'}, dimensions={0} | all-to-all | bytes 1638400 | tf_op jit(solution)/shard_map/all_to_all | solution.py:49
  646.5 4.5 all-to-all-start.3
  652.3 2.5 all_to_all.85
  656.6 2.8 all_to_all.101
  659.4 9.6 %all-to-all-done.3 = f32[8,160,160]{2,1,0:T(8,128)S(1)} async-done(((f32[8,160,160]{2,1,0:T(8,128)}), f32[8,160,160]{2,1,0:T(8,128)S(1)}, u32[]{:S(2)}, u32[]{:S(2)}) %all-to-all-start.3) | async-done | bytes 819232 | tf_op jit(solution)/shard_map/all_to_all | solution.py:48
  (51 shorter events, 32.4 us)
Async XLA Ops:
  7.2 245.1 %all-gather.5.cloned.1.call-start = ((), (), s32[]{:S(2)}) async-start(), calls=%async_computation.7 | async-start | bytes 10813440 | tf_op jit(solution)/shard_map/all_gather | solution.py:71
  7.9 244.4 %copy-start.2 = (bf16[1,160,1280]{2,1,0:T(8,128)(2,1)S(1)}, bf16[1,160,1280]{2,1,0:T(8,128)(2,1)}, u32[]{:S(2)}) copy-start(bf16[1,160,1280]{2,1,0:T(8,128)(2,1)} %param.12) | copy-start | bytes 1228804
  7.9 292.8 %all-gather.7.cloned.1.call-start = ((), (), s32[]{:S(2)}) async-start(), calls=%async_computation.8 | async-start | bytes 3145728 | tf_op jit(solution)/shard_map/all_gather | solution.py:79
  10.8 390.2 %all-reduce.3.cloned.1.call-start = ((), (), s32[]{:S(2)}) async-start(), calls=%async_computation.6 | async-start | bytes 5242880 | tf_op jit(solution)/shard_map/psum | solution.py:78
  261.3 0.7 copy-start.4
  261.3 0.7 copy-start.5
  261.3 1.3 copy-start.3
  519.9 34.3 %copy-start.1 = (f32[1,160,1280]{2,1,0:T(8,128)S(1)}, f32[1,160,1280]{2,1,0:T(8,128)}, u32[]{:S(2)}) copy-start(f32[1,160,1280]{2,1,0:T(8,128)} %get-tuple-element.12) | copy-start | bytes 2457604
  521.7 40.8 %all-to-all-start = ((bf16[8,2,12800]{2,1,0:T(2,128)(2,1)}), bf16[8,2,12800]{2,1,0:T(2,128)(2,1)S(1)}, u32[]{:S(2)}, u32[]{:S(2)}) async-start(bf16[8,2,12800]{2,1,0:T(2,128)(2,1)} %reshape.82), calls=%async_computation | async-start | bytes 819200 | tf_op jit(solution)/shard_map/all_to_all | solution.py:33
  556.4 10.4 %copy-start.6 = (s32[8,1]{0,1:T(1,128)S(1)}, s32[8,1]{0,1:T(1,128)}, u32[]{:S(2)}) copy-start(s32[8,1]{0,1:T(1,128)} %param.19) | copy-start | bytes 100
  556.4 10.4 %copy-start = (f32[1,160,1280]{2,1,0:T(8,128)S(1)}, f32[1,160,1280]{2,1,0:T(8,128)}, u32[]{:S(2)}) copy-start(f32[1,160,1280]{2,1,0:T(8,128)} %get-tuple-element.10) | copy-start | bytes 2457604
  562.5 22.3 %all-to-all-start.2 = ((f32[1,160,1280]{1,0,2:T(1,128)}), f32[1,160,1280]{1,0,2:T(1,128)S(1)}, u32[]{:S(2)}, u32[]{:S(2)}) async-start(f32[1,160,1280]{1,0,2:T(1,128)} %copy.78), calls=%async_computation.2 | async-start | bytes 2621440 | tf_op jit(solution)/shard_map/all_to_all | solution.py:42
  584.7 22.3 %all-to-all-start.4 = ((f32[1,160,1280]{1,0,2:T(1,128)}), f32[1,160,1280]{1,0,2:T(1,128)S(1)}, u32[]{:S(2)}, u32[]{:S(2)}) async-start(f32[1,160,1280]{1,0,2:T(1,128)} %copy.82), calls=%async_computation.4 | async-start | bytes 2621440 | tf_op jit(solution)/shard_map/all_to_all | solution.py:43
  607.0 17.0 %all-to-all-start.1 = ((bf16[8,160,160]{2,1,0:T(8,128)(2,1)}), bf16[8,160,160]{2,1,0:T(8,128)(2,1)S(1)}, u32[]{:S(2)}, u32[]{:S(2)}) async-start(bf16[8,160,160]{2,1,0:T(8,128)(2,1)} %broadcast_select_fusion.2), calls=%async_computation.1 | async-start | bytes 1310720 | tf_op jit(solution)/shard_map/all_to_all | solution.py:35
  646.5 22.4 %all-to-all-start.3 = ((f32[8,160,160]{2,1,0:T(8,128)}), f32[8,160,160]{2,1,0:T(8,128)S(1)}, u32[]{:S(2)}, u32[]{:S(2)}) async-start(f32[8,160,160]{2,1,0:T(8,128)} %get-tuple-element.16), calls=%async_computation.3 | async-start | bytes 2621440 | tf_op jit(solution)/shard_map/all_to_all | solution.py:48
Sparse Core Ops, SparseCore 0:
  10.1 242.1 all-gather.4
  254.4 46.2 all-gather.6
  303.6 97.3 all-reduce.2
where the time goes:
time: 679 us; the launch traced here: 678 us
  waiting for transfers between devices  416 us (61%)
  blocking collectives  117 us (17%)
  starting transfers between devices  50.2 us (7%)
  local copies, waits for them, and re-layouts  45.3 us (7%)
  matrix products  19.6 us (3%)
  other arithmetic  15.1 us (2%)
  between operations  13.9 us (2%)
    all_gather x1, waiting for transfers between devices, body(): gathered = lax.all_gather(local_rows, 'dp', axis=0, tiled=True)  241 us
    psum x1, blocking collectives, weight_gradient(): lax.psum((jnp.sum(outputs * outputs, axis=0), jnp.sum(goal * outputs, axi...  94.9 us
    psum x1, waiting for transfers between devices, body(): outputs = lax.psum(partial_out, 'tensor')  94.2 us
    all_gather x1, waiting for transfers between devices, body(): goal_full = lax.all_gather(goal_local, 'tensor', axis=1, tiled=True)  38.2 us
    all_to_all x1, starting transfers between devices, route_weights(): lax.all_to_all(shaped, 'member', split_axis=2, concat_axis=0, tiled=True)  32.6 us
    all_to_all x1, blocking collectives, route_moments(): lax.all_to_all(second_picked, 'member', split_axis=0, concat_axis=2, tile...  22.5 us
    all_to_all x1, waiting for transfers between devices, route_moments(): lax.all_to_all(first_shaped, 'member', split_axis=2, concat_axis=0, tiled...  15.7 us
  transfers between devices with their start and end apart: 8, of which 7 were waited for; matrix products, arithmetic and copies ran while one was open for 7% of the time, Pallas kernels for 0%

commit v1 on v0

v1 whole, which is shorter than its diff:
```python
import math

import jax
import jax.numpy as jnp
from jax import lax
from jax.experimental import pallas as pl
from jax.experimental.pallas import tpu as pltpu
from jax.sharding import PartitionSpec as P

D = 5120
HW = 2560
MEMBERS = 8
ZN = 16
YN = 4
ROWS = 160
COLS = 1280
HALF = 80
TOK = 64
SLOTS = 8
CB = 256
NB = COLS // CB
SCALING = 1.0 / math.sqrt(HW)

beta_one = 0.9
beta_two = 0.95
norm_eps = 1e-05
adam_eps = 1e-08

MESH = pl.DeviceIdType.MESH
F32 = jnp.float32
BF16 = jnp.bfloat16


def remote(src, dst, send_sem, recv_sem, device):
    return pltpu.make_async_remote_copy(
        src_ref=src,
        dst_ref=dst,
        send_sem=send_sem,
        recv_sem=recv_sem,
        device_id=device,
        device_id_type=MESH,
    )


def gradient_kernel(
    ctx,
    w,
    m,
    v,
    tgt,
    ids,
    gall,
    wall,
    mall,
    vall,
    xbuf,
    wbuf,
    tbuf,
    eye,
    yt,
    gt,
    dyt,
    stat,
    early,
    late_out,
    late,
    tot,
    pbuf,
    r1,
    r2,
    rout,
    loc,
    in_s,
    in_r,
    z_s,
    z_r,
    e_s,
    e_r,
    l_s,
    l_r,
    st_s,
    st_r,
    x_s,
    x_r,
    y_s,
    y_r,
    y_l,
):
    mem = lax.axis_index("member")
    dp = lax.axis_index("dp")
    ten = lax.axis_index("tensor")
    yy, core = mem // 2, mem % 2
    zz, xl = dp // 2, dp % 2

    def at_z(k):
        return (mem, lax.rem(zz + k, ZN) * 2 + xl, ten)

    def member_at(k):
        return lax.rem(yy + k, YN) * 2 + core

    right, left = at_z(1), at_z(ZN - 1)
    dev_a = (mem, zz * 2 + 1 - xl, ten)
    dev_b = (mem, zz * 2 + 1 - xl, 1 - ten)
    dev_c = (mem, dp, 1 - ten)
    up_m, down_m, far_m = member_at(1), member_at(YN - 1), member_at(2)
    sib_m = yy * 2 + 1 - core
    up, down, sib = (up_m, dp, ten), (down_m, dp, ten), (sib_m, dp, ten)

    own_rows = ctx.at[pl.ds(pl.multiple_of(ten * TOK, TOK), TOK)]
    other_rows = ctx.at[pl.ds(pl.multiple_of((1 - ten) * TOK, TOK), TOK)]

    locals_ = [
        pltpu.make_async_copy(own_rows, xbuf.at[0, 0, 0], loc.at[0]),
        pltpu.make_async_copy(w, wbuf.at[0, 0], loc.at[1]),
        pltpu.make_async_copy(tgt.at[:, xl], tbuf.at[0], loc.at[2]),
        pltpu.make_async_copy(w, wall.at[mem], loc.at[3]),
        pltpu.make_async_copy(m, mall.at[mem], loc.at[4]),
        pltpu.make_async_copy(v, vall.at[mem], loc.at[5]),
    ]
    for copy in locals_:
        copy.start()

    barrier = pltpu.get_barrier_semaphore()

    def greet(k, _):
        pl.semaphore_signal(barrier, inc=1, device_id=at_z(k), device_id_type=MESH)
        return 0

    lax.fori_loop(1, ZN, greet, 0)
    for device in (dev_a, dev_b, dev_c, up, down, sib):
        pl.semaphore_signal(barrier, inc=1, device_id=device, device_id_type=MESH)
    pl.semaphore_wait(barrier, ZN - 1 + 6)

    swap = remote(other_rows, xbuf.at[1, 0, 0], in_s.at[0], in_r.at[0], dev_c)
    swap.start()

    def ring(h, s, d):
        dst = xbuf.at[h, lax.rem(s + 1, SLOTS), d if d else s // (SLOTS - 1)]
        return remote(
            xbuf.at[h, s, d],
            dst,
            z_s.at[d, h, s],
            z_r.at[d, h, lax.rem(s + 1, SLOTS)],
            left if d else right,
        )

    def first(h, d, src):
        return remote(
            src, xbuf.at[h, 1, d], z_s.at[d, h, 0], z_r.at[d, h, 1], left if d else right
        )

    for d in (0, 1):
        first(0, d, own_rows).start()
    inputs = [
        remote(w, wbuf.at[0, 1], in_s.at[1], in_r.at[1], dev_a),
        remote(w, wbuf.at[1, 1], in_s.at[2], in_r.at[2], dev_b),
        remote(w, wbuf.at[1, 0], in_s.at[3], in_r.at[3], dev_c),
        remote(tgt.at[:, 1 - xl], tbuf.at[1], in_s.at[4], in_r.at[4], dev_a),
    ]
    for copy in inputs:
        copy.start()

    state = [(w, wall), (m, mall), (v, vall)]

    def state_first(i, src, dst):
        return [
            remote(src, dst.at[mem], st_s.at[i, 0], st_r.at[i, 0], up),
            remote(src, dst.at[mem], st_s.at[i, 1], st_r.at[i, 1], down),
            remote(src, dst.at[mem], st_s.at[i, 2], st_r.at[i, 2], sib),
        ]

    def state_on(i, dst):
        low, high = pl.ds(0, HALF), pl.ds(HALF, HALF)
        return [
            remote(dst.at[down_m, low], dst.at[down_m, low], st_s.at[i, 3], st_r.at[i, 3], up),
            remote(dst.at[up_m, high], dst.at[up_m, high], st_s.at[i, 4], st_r.at[i, 4], down),
            remote(dst.at[down_m], dst.at[down_m], st_s.at[i, 5], st_r.at[i, 5], sib),
            remote(dst.at[up_m], dst.at[up_m], st_s.at[i, 6], st_r.at[i, 6], sib),
        ]

    def state_last(i, dst):
        return remote(dst.at[far_m], dst.at[far_m], st_s.at[i, 7], st_r.at[i, 7], sib)

    for i, (src, dst) in enumerate(state):
        for copy in state_first(i, src, dst):
            copy.start()

    eye[...] = (
        lax.broadcasted_iota(jnp.int32, (ROWS, ROWS), 0)
        == lax.broadcasted_iota(jnp.int32, (ROWS, ROWS), 1)
    ).astype(BF16)
    stat[...] = jnp.zeros_like(stat)
    lane = lax.broadcasted_iota(jnp.int32, (1, 2 * TOK), 1)
    low_lanes = lane < TOK

    swap.wait_recv()
    for d in (0, 1):
        first(1, d, xbuf.at[1, 0, 0]).start()
    for copy in locals_:
        copy.wait()

    def chunks_of(s):
        one = lax.rem(zz - s + ZN, ZN)
        two = lax.rem(zz + jnp.where(s == 0, SLOTS, s), ZN)
        return one, two

    def project(s):
        one, two = chunks_of(s)
        total = None
        for h in (0, 1):
            part = lax.dot_general(
                wbuf[h].reshape(2 * ROWS, COLS),
                xbuf[h, s].reshape(2 * TOK, COLS),
                (((1,), (1,)), ((), ())),
                preferred_element_type=F32,
            )
            total = part if total is None else total + part
        out = total * SCALING
        yt[s] = out
        goal = jnp.concatenate(
            [
                lax.dot_general(
                    eye[...],
                    jnp.concatenate([tbuf[side, one], tbuf[side, two]], axis=0),
                    (((1,), (1,)), ((), ())),
                    preferred_element_type=F32,
                )
                for side in (0, 1)
            ],
            axis=0,
        )
        gt[s] = goal
        squares = jnp.sum(out * out, axis=0, keepdims=True)
        crosses = jnp.sum(goal * out, axis=0, keepdims=True)
        row_one = jnp.where(low_lanes, squares, pltpu.roll(crosses, TOK, 1))
        row_two = jnp.where(low_lanes, pltpu.roll(squares, TOK, 1), crosses)
        return one, two, row_one, row_two

    def project_early(s, _):
        one, two, row_one, row_two = project(s)
        stat[pl.ds(one, 1), :] = row_one
        stat[pl.ds(two, 1), :] = row_two
        return 0

    def done_by(s):
        return jnp.minimum(jnp.maximum(2 * (s - 3), 0), SLOTS - 1)

    def gather_step(s, _):
        for h in (0, 1):
            for d in (0, 1):
                remote(
                    xbuf.at[h, s, d], xbuf.at[h, s, d], z_s.at[d, h, s], z_r.at[d, h, s], right
                ).wait_recv()
                if d == h:
                    ring(h, s, d).start()
                else:

                    @pl.when(s < SLOTS - 1)
                    def _():
                        ring(h, s, d).start()

        @pl.when(s == 4)
        def _():
            for copy in inputs:
                copy.wait_recv()

        lax.fori_loop(done_by(s - 1) + 1, done_by(s) + 1, project_early, 0)
        return 0

    lax.fori_loop(1, SLOTS, gather_step, 0)

    def early_copy(k):
        return remote(stat, early.at[zz], e_s.at[k], e_r.at[zz], at_z(k))

    def late_copy(k):
        return remote(late_out, late.at[zz], l_s.at[k], l_r.at[zz], at_z(k))

    def send_early(k, _):
        early_copy(k).start()
        return 0

    lax.fori_loop(1, ZN, send_early, 0)
    early[zz] = stat[...]

    for h in (0, 1):
        remote(
            xbuf.at[h, 0, 1], xbuf.at[h, 0, 1], z_s.at[h, h, 0], z_r.at[h, h, 0], right
        ).wait_recv()
    _, _, row_one, row_two = project(0)
    late_out[pl.ds(0, 1), :] = row_one
    late_out[pl.ds(1, 1), :] = row_two

    def send_late(k, _):
        late_copy(k).start()
        return 0

    lax.fori_loop(1, ZN, send_late, 0)
    late[zz] = late_out[...]

    for i, (src, dst) in enumerate(state):
        for copy in state_first(i, src, dst):
            copy.wait_recv()
        for copy in state_on(i, dst):
            copy.start()

    def take_early(k, total):
        src = lax.rem(zz + k, ZN)
        remote(stat, early.at[src], e_s.at[k], e_r.at[src], right).wait_recv()
        return total + early[src]

    tot[...] = lax.fori_loop(1, ZN, take_early, stat[...])

    def take_late(k, _):
        src = lax.rem(zz + k, ZN)
        remote(late_out, late.at[src], l_s.at[k], l_r.at[src], right).wait_recv()
        return 0

    lax.fori_loop(1, ZN, take_late, 0)

    def add_late(c, _):
        opposite = lax.rem(c + SLOTS, ZN)
        tot[pl.ds(c, 1), :] = (
            tot[pl.ds(c, 1), :] + late[c, pl.ds(0, 1), :] + late[opposite, pl.ds(1, 1), :]
        )
        return 0

    lax.fori_loop(0, ZN, add_late, 0)

    def window_mask(c):
        row = ids[pl.ds(2 * c + xl, 1), :]
        return jnp.where(row != 0, 1.0, 0.0)

    def out_gradient(s, _):
        one, two = chunks_of(s)
        row_one, row_two = tot[pl.ds(one, 1), :], tot[pl.ds(two, 1), :]
        squares = jnp.where(low_lanes, row_one, pltpu.roll(row_two, TOK, 1))
        crosses = jnp.where(low_lanes, pltpu.roll(row_one, TOK, 1), row_two)
        mask_one, mask_two = window_mask(one), window_mask(two)
        first_half = jnp.where(low_lanes, mask_one, pltpu.roll(mask_two, TOK, 1))
        second_half = jnp.where(low_lanes, pltpu.roll(mask_one, TOK, 1), mask_two)
        mask = jnp.where(ten == 0, first_half, second_half)
        inverse = lax.rsqrt(squares / D + norm_eps)
        projection = mask * (inverse * inverse * squares - inverse * crosses) / D
        normed = yt[s] * inverse
        hidden = mask * (normed - gt[s])
        grad_out = inverse * (hidden - normed * projection)
        dyt[:, pl.ds(pl.multiple_of(s * 2 * TOK, 2 * TOK), 2 * TOK)] = grad_out.astype(BF16)
        return 0

    lax.fori_loop(0, SLOTS, out_gradient, 0)

    low, high = pl.ds(0, HALF), pl.ds(HALF, HALF)

    def hop_one(j):
        return [
            remote(pbuf.at[j, 1, 0, low], r1.at[0, j], x_s.at[0, j], x_r.at[0, j], dev_a),
            remote(pbuf.at[j, 1, 0, high], r1.at[1, j], x_s.at[1, j], x_r.at[1, j], dev_b),
        ]

    def hop_two(j):
        return [
            remote(pbuf.at[j, 0, 1], r2.at[0, j], x_s.at[2, j], x_r.at[2, j], dev_a),
            remote(pbuf.at[j, 1, 1], r2.at[1, j], x_s.at[3, j], x_r.at[3, j], dev_b),
        ]

    def y_local(j):
        return pltpu.make_async_copy(rout.at[j], gall.at[mem, j], y_l.at[j])

    def y_first(j):
        return [
            remote(rout.at[j], gall.at[mem, j], y_s.at[0, j], y_r.at[0, j], up),
            remote(rout.at[j], gall.at[mem, j], y_s.at[1, j], y_r.at[1, j], down),
            remote(rout.at[j], gall.at[mem, j], y_s.at[2, j], y_r.at[2, j], sib),
        ]

    def y_on(j):
        one, two = gall.at[down_m, j], gall.at[up_m, j]
        return [
            remote(one.at[low], one.at[low], y_s.at[3, j], y_r.at[3, j], up),
            remote(two.at[high], two.at[high], y_s.at[4, j], y_r.at[4, j], down),
            remote(one, one, y_s.at[5, j], y_r.at[5, j], sib),
            remote(two, two, y_s.at[6, j], y_r.at[6, j], sib),
        ]

    def y_last(j):
        return remote(gall.at[far_m, j], gall.at[far_m, j], y_s.at[7, j], y_r.at[7, j], sib)

    def far_halves(ref, sems):
        return [
            remote(ref.at[low], ref.at[low], sems[0], sems[1], up),
            remote(ref.at[high], ref.at[high], sems[2], sems[3], up),
        ]

    def stage(step, behind, run):
        j = step - behind

        @pl.when(jnp.logical_and(j >= 0, j < NB))
        def _():
            run(j)

    def multiply(j):
        cols = pl.ds(pl.multiple_of(j * CB, CB), CB)
        for h in (1, 0):
            part = jnp.dot(
                dyt[...],
                xbuf[h, :, :, :, cols].reshape(2 * SLOTS * TOK, CB),
                preferred_element_type=F32,
            )
            pbuf[j, h] = (part * SCALING).reshape(2, ROWS, CB)
        for copy in hop_one(j):
            copy.start()

    def add_one(j):
        for copy in hop_one(j):
            copy.wait_recv()
        pbuf[j, 1, 1, low] = pbuf[j, 1, 1, low] + r1[0, j]
        pbuf[j, 0, 1, high] = pbuf[j, 0, 1, high] + r1[1, j]
        for copy in hop_two(j):
            copy.start()

    def add_two(j):
        for copy in hop_two(j):
            copy.wait_recv()
        rout[j] = pbuf[j, 0, 0] + r2[0, j] + r2[1, j]
        y_local(j).start()
        for copy in y_first(j):
            copy.start()

    def pass_on(j):
        for copy in y_first(j):
            copy.wait_recv()
        for copy in y_on(j):
            copy.start()

    def pass_last(j):
        for copy in y_on(j):
            copy.wait_recv()
        y_last(j).start()

    def finish(j):
        y_last(j).wait_recv()
        y_local(j).wait()
        for copy in hop_one(j) + hop_two(j) + y_first(j) + y_on(j) + [y_last(j)]:
            copy.wait_send()

    def pipeline_step(step, _):
        for behind, run in enumerate((multiply, add_one, add_two, pass_on, pass_last, finish)):
            stage(step, behind, run)
        return 0

    lax.fori_loop(0, NB + 5, pipeline_step, 0)

    for i, (src, dst) in enumerate(state):
        for copy in state_on(i, dst):
            copy.wait_recv()
        state_last(i, dst).start()
    for i, (src, dst) in enumerate(state):
        state_last(i, dst).wait_recv()
        for copy in state_first(i, src, dst) + state_on(i, dst) + [state_last(i, dst)]:
            copy.wait_send()
    swap.wait_send()
    for copy in inputs:
        copy.wait_send()
    for d in (0, 1):
        first(0, d, own_rows).wait_send()
        first(1, d, xbuf.at[1, 0, 0]).wait_send()

    def drain_ring(s, _):
        for h in (0, 1):
            for d in (0, 1):
                if d == h:
                    ring(h, s, d).wait_send()
                else:

                    @pl.when(s < SLOTS - 1)
                    def _():
                        ring(h, s, d).wait_send()

        return 0

    lax.fori_loop(1, SLOTS, drain_ring, 0)

    def drain_stats(k, _):
        early_copy(k).wait_send()
        late_copy(k).wait_send()
        return 0

    lax.fori_loop(1, ZN, drain_stats, 0)


def gather_gradients(ctx, w, m, v, tgt, ids):
    anywhere = pl.BlockSpec(memory_space=pl.ANY)
    dma = pltpu.SemaphoreType.DMA
    vmem = pltpu.VMEM
    return pl.pallas_call(
        gradient_kernel,
        out_shape=(
            jax.ShapeDtypeStruct((MEMBERS, NB, ROWS, CB), F32),
            jax.ShapeDtypeStruct((MEMBERS, ROWS, COLS), BF16),
            jax.ShapeDtypeStruct((MEMBERS, ROWS, COLS), F32),
            jax.ShapeDtypeStruct((MEMBERS, ROWS, COLS), F32),
        ),
        in_specs=[anywhere] * 5 + [pl.BlockSpec(memory_space=pltpu.VMEM)],
        out_specs=(anywhere,) * 4,
        scratch_shapes=[
            vmem((2, SLOTS, 2, TOK, COLS), BF16),
            vmem((2, 2, ROWS, COLS), BF16),
            vmem((2, ZN, TOK, ROWS), BF16),
            vmem((ROWS, ROWS), BF16),
            vmem((SLOTS, 2 * ROWS, 2 * TOK), F32),
            vmem((SLOTS, 2 * ROWS, 2 * TOK), F32),
            vmem((2 * ROWS, SLOTS * 2 * TOK), BF16),
            vmem((ZN, 2 * TOK), F32),
            vmem((ZN, ZN, 2 * TOK), F32),
            vmem((2, 2 * TOK), F32),
            vmem((ZN, 2, 2 * TOK), F32),
            vmem((ZN, 2 * TOK), F32),
            vmem((NB, 2, 2, ROWS, CB), F32),
            vmem((2, NB, HALF, CB), F32),
            vmem((2, NB, ROWS, CB), F32),
            vmem((NB, ROWS, CB), F32),
            dma((6,)),
            dma((5,)),
            dma((5,)),
            dma((2, 2, SLOTS)),
            dma((2, 2, SLOTS)),
            dma((ZN,)),
            dma((ZN,)),
            dma((ZN,)),
            dma((ZN,)),
            dma((3, 8)),
            dma((3, 8)),
            dma((4, NB)),
            dma((4, NB)),
            dma((8, NB)),
            dma((8, NB)),
            dma((NB,)),
        ],
        compiler_params=pltpu.CompilerParams(
            collective_id=0, has_side_effects=True, vmem_limit_bytes=56 * 1024 * 1024
        ),
        cost_estimate=pl.CostEstimate(
            flops=4 * 1024 * HW * 2 * ROWS, bytes_accessed=20_000_000, transcendentals=0
        ),
    )(ctx, w, m, v, tgt, ids)


def update_kernel(pick, rate_of, level_of, g, w, m, v, new_w, new_m, new_v):
    p = pick[0]
    level = jnp.full((8, CB), level_of[p].astype(F32), F32)
    step_size = (rate_of[p] * 2.0 ** ((level - 4.0) / 4.0))[:1]
    gradient = g[0, 0]
    first = beta_one * m[0] + (1.0 - beta_one) * gradient
    second = beta_two * v[0] + (1.0 - beta_two) * gradient * gradient
    new_w[...] = (w[0].astype(F32) - step_size * first / (jnp.sqrt(second) + adam_eps)).astype(BF16)
    new_m[...] = first
    new_v[...] = second


def update(pick, base_lr, perturb_index, gall, wall, mall, vall):
    def member_block(j, pick, rate, level):
        return (pick[0], 0, j)

    def own_block(j, pick, rate, level):
        return (0, j)

    return pl.pallas_call(
        update_kernel,
        out_shape=(
            jax.ShapeDtypeStruct((ROWS, COLS), BF16),
            jax.ShapeDtypeStruct((ROWS, COLS), F32),
            jax.ShapeDtypeStruct((ROWS, COLS), F32),
        ),
        grid_spec=pltpu.PrefetchScalarGridSpec(
            num_scalar_prefetch=3,
            grid=(NB,),
            in_specs=[
                pl.BlockSpec((1, 1, ROWS, CB), lambda j, pick, rate, level: (pick[0], j, 0, 0)),
                pl.BlockSpec((1, ROWS, CB), member_block),
                pl.BlockSpec((1, ROWS, CB), member_block),
                pl.BlockSpec((1, ROWS, CB), member_block),
            ],
            out_specs=(
                pl.BlockSpec((ROWS, CB), own_block),
                pl.BlockSpec((ROWS, CB), own_block),
                pl.BlockSpec((ROWS, CB), own_block),
            ),
        ),
    )(pick, base_lr, perturb_index, gall, wall, mall, vall)


def body(
    context,
    out_weight,
    first_moment,
    second_moment,
    target,
    token_ids,
    base_lr,
    perturb_index,
    partner,
):
    gall, wall, mall, vall = gather_gradients(
        context[0, 0],
        out_weight[0],
        first_moment[0],
        second_moment[0],
        target[0].reshape(ZN, 2, TOK, ROWS),
        token_ids[0],
    )
    pick = lax.dynamic_slice(partner[:, 0], (lax.axis_index("member"),), (1,))
    new_weight, new_first, new_second = update(pick, base_lr, perturb_index, gall, wall, mall, vall)
    return (new_weight[None], new_first[None], new_second[None])


def solution(mesh):
    return jax.shard_map(
        body,
        mesh=mesh,
        in_specs=(
            P("member", "dp", None, "tensor"),
            P("member", "dp", "tensor"),
            P("member", "dp", "tensor"),
            P("member", "dp", "tensor"),
            P("member", None, "tensor", "dp"),
            P("member", None, None),
            P(),
            P(),
            P(None, "dp"),
        ),
        out_specs=(
            P("member", "dp", "tensor"),
            P("member", "dp", "tensor"),
            P("member", "dp", "tensor"),
        ),
        check_vma=False,
    )
```

time: 679 us -> 195 us (0.29)
  waiting for transfers between devices: 416 us -> 0 us
  Pallas kernels: 0 us -> 193 us
  blocking collectives: 117 us -> 0 us
  starting transfers between devices: 50.2 us -> 0 us
  local copies, waits for them, and re-layouts: 45.3 us -> 1.2 us
  matrix products: 19.6 us -> 0 us
  other arithmetic: 15.1 us -> 0 us
  between operations: 13.9 us -> 0.65 us
    all_gather x2 -> x0, waiting for transfers between devices: 280 us -> none  [the longest x1 241 us: body(): gathered = lax.all_gather(local_rows, 'dp', axis=0, tiled=True)]
    pallas_call x0 -> x2, Pallas kernels: none -> 193 us  [the longest x1 187 us: gather_gradients(): pl.pallas_call(gradient_kernel, out_shape=(jax.ShapeDtypeStruct((MEMBERS,...]
    psum x1 -> x0, blocking collectives: 94.9 us -> none  [weight_gradient(): lax.psum((jnp.sum(outputs * outputs, axis=0), jnp.sum(goal * outputs, axi...]
    psum x1 -> x0, waiting for transfers between devices: 94.2 us -> none  [body(): outputs = lax.psum(partial_out, 'tensor')]
    all_to_all x5 -> x0, starting transfers between devices: 50.1 us -> none  [the longest x1 32.6 us: route_weights(): lax.all_to_all(shaped, 'member', split_axis=2, concat_axis=0, tiled=True)]
    all_to_all x5 -> x0, waiting for transfers between devices: 41.7 us -> none  [the longest x1 15.7 us: route_moments(): lax.all_to_all(first_shaped, 'member', split_axis=2, concat_axis=0, tiled...]
    all_to_all x1 -> x0, blocking collectives: 22.5 us -> none  [route_moments(): lax.all_to_all(second_picked, 'member', split_axis=0, concat_axis=2, tile...]
    dot_general x2 -> x0, matrix products: 19.6 us -> none  [the longest x1 10.6 us: weight_gradient(): jnp.dot(grad_out, gathered, preferred_element_type=jnp.float32) * scaling]
  transfers between devices with their start and end apart: 8 -> 0, of which waited for: 7 -> 0; matrix products, arithmetic and copies ran while one was open for 7% -> 0% of each run, Pallas kernels for 0% -> 0%
where the time goes in v1:
time: 195 us
  Pallas kernels  193 us (99%)
    pallas_call x1, Pallas kernels, gather_gradients(): pl.pallas_call(gradient_kernel, out_shape=(jax.ShapeDtypeStruct((MEMBERS,...  187 us
    pallas_call x1, Pallas kernels, update(): pl.pallas_call(update_kernel, out_shape=(jax.ShapeDtypeStruct((ROWS, COLS...  5.94 us

profile of v1, /device:TPU:1, one launch (start us, length us, event | category | flops | bytes accessed | tf_op | source)
XLA Modules:
  0.0 195.0 jit_solution(16046878266236039387)
XLA Ops:
  0.6 0.0 copy-start
  0.6 0.6 copy-done
  1.3 0.6 constant_dynamic-slice_fusion
  1.8 187.2 %shard_map.112 = (f32[8,5,160,256]{3,2,1,0:T(8,128)}, bf16[8,160,1280]{2,1,0:T(8,128)(2,1)}, f32[8,160,1280]{2,1,0:T(8,128)}, f32[8,160,1280]{2,1,0:T(8,128)}) custom-call(bf16[128,1280]{1,0:T(8,128)(2,1)} %bitcast.17, bf16[160,1280]{1,0:T(8,128)(2,1)} %bitcast.15, f32[160,1280]{1,0:T(8,128)} %bitcast.11, f32[160,1280]{1,0:T(8,128)} %bitcast.12, ...), custom_call_target="tpu_custom_call" | custom-call | flops 3355443200 | bytes 20000000 | tf_op jit(solution)/shard_map/pallas_call | solution.py:495
  189.0 5.9 %shard_map.113 = (bf16[160,1280]{1,0:T(8,128)(2,1)}, f32[160,1280]{1,0:T(8,128)}, f32[160,1280]{1,0:T(8,128)}) custom-call(s32[1]{0:T(128)} %bitcast.pick, f32[8]{0:T(128)} %rate_of.1, s32[8]{0:T(128)} %level_of.1, f32[8,5,160,256]{3,2,1,0:T(8,128)} %get-tuple-element.10.g, bf16[8,160,1280]{2,1,0:T(8,128)(2,1)} %get-tuple-element.11.w, ...), custom_call_target="tpu_custom_call" | custom-call | tf_op jit(solution)/shard_map/pallas_call | solution.py:567
Async XLA Ops:
  0.6 0.7 copy-start

commit v2 on v1

--- a/solution.py
+++ b/solution.py
@@ -126,10 +126,11 @@
         pl.semaphore_signal(barrier, inc=1, device_id=at_z(k), device_id_type=MESH)
         return 0
 
-    lax.fori_loop(1, ZN, greet, 0)
-    for device in (dev_a, dev_b, dev_c, up, down, sib):
-        pl.semaphore_signal(barrier, inc=1, device_id=device, device_id_type=MESH)
-    pl.semaphore_wait(barrier, ZN - 1 + 6)
+    with jax.named_scope("entry_barrier"):
+        lax.fori_loop(1, ZN, greet, 0)
+        for device in (dev_a, dev_b, dev_c, up, down, sib):
+            pl.semaphore_signal(barrier, inc=1, device_id=device, device_id_type=MESH)
+        pl.semaphore_wait(barrier, ZN - 1 + 6)
 
     swap = remote(other_rows, xbuf.at[1, 0, 0], in_s.at[0], in_r.at[0], dev_c)
     swap.start()
@@ -193,11 +194,13 @@
     lane = lax.broadcasted_iota(jnp.int32, (1, 2 * TOK), 1)
     low_lanes = lane < TOK
 
-    swap.wait_recv()
+    with jax.named_scope("swap_wait"):
+        swap.wait_recv()
     for d in (0, 1):
         first(1, d, xbuf.at[1, 0, 0]).start()
-    for copy in locals_:
-        copy.wait()
+    with jax.named_scope("local_wait"):
+        for copy in locals_:
+            copy.wait()
 
     def chunks_of(s):
         one = lax.rem(zz - s + ZN, ZN)
@@ -248,9 +251,10 @@
     def gather_step(s, _):
         for h in (0, 1):
             for d in (0, 1):
-                remote(
-                    xbuf.at[h, s, d], xbuf.at[h, s, d], z_s.at[d, h, s], z_r.at[d, h, s], right
-                ).wait_recv()
+                with jax.named_scope("ring_wait"):
+                    remote(
+                        xbuf.at[h, s, d], xbuf.at[h, s, d], z_s.at[d, h, s], z_r.at[d, h, s], right
+                    ).wait_recv()
                 if d == h:
                     ring(h, s, d).start()
                 else:
@@ -261,10 +265,12 @@
 
         @pl.when(s == 4)
         def _():
-            for copy in inputs:
-                copy.wait_recv()
-
-        lax.fori_loop(done_by(s - 1) + 1, done_by(s) + 1, project_early, 0)
+            with jax.named_scope("inputs_wait"):
+                for copy in inputs:
+                    copy.wait_recv()
+
+        with jax.named_scope("project_slots"):
+            lax.fori_loop(done_by(s - 1) + 1, done_by(s) + 1, project_early, 0)
         return 0
 
     lax.fori_loop(1, SLOTS, gather_step, 0)
@@ -282,11 +288,13 @@
     lax.fori_loop(1, ZN, send_early, 0)
     early[zz] = stat[...]
 
-    for h in (0, 1):
-        remote(
-            xbuf.at[h, 0, 1], xbuf.at[h, 0, 1], z_s.at[h, h, 0], z_r.at[h, h, 0], right
-        ).wait_recv()
-    _, _, row_one, row_two = project(0)
+    with jax.named_scope("ring_last_wait"):
+        for h in (0, 1):
+            remote(
+                xbuf.at[h, 0, 1], xbuf.at[h, 0, 1], z_s.at[h, h, 0], z_r.at[h, h, 0], right
+            ).wait_recv()
+    with jax.named_scope("project_last"):
+        _, _, row_one, row_two = project(0)
     late_out[pl.ds(0, 1), :] = row_one
     late_out[pl.ds(1, 1), :] = row_two
 
@@ -297,25 +305,28 @@
     lax.fori_loop(1, ZN, send_late, 0)
     late[zz] = late_out[...]
 
-    for i, (src, dst) in enumerate(state):
-        for copy in state_first(i, src, dst):
-            copy.wait_recv()
-        for copy in state_on(i, dst):
-            copy.start()
+    with jax.named_scope("state_first_wait"):
+        for i, (src, dst) in enumerate(state):
+            for copy in state_first(i, src, dst):
+                copy.wait_recv()
+            for copy in state_on(i, dst):
+                copy.start()
 
     def take_early(k, total):
         src = lax.rem(zz + k, ZN)
         remote(stat, early.at[src], e_s.at[k], e_r.at[src], right).wait_recv()
         return total + early[src]
 
-    tot[...] = lax.fori_loop(1, ZN, take_early, stat[...])
+    with jax.named_scope("early_sums"):
+        tot[...] = lax.fori_loop(1, ZN, take_early, stat[...])
 
     def take_late(k, _):
         src = lax.rem(zz + k, ZN)
         remote(late_out, late.at[src], l_s.at[k], l_r.at[src], right).wait_recv()
         return 0
 
-    lax.fori_loop(1, ZN, take_late, 0)
+    with jax.named_scope("late_sums"):
+        lax.fori_loop(1, ZN, take_late, 0)
 
     def add_late(c, _):
         opposite = lax.rem(c + SLOTS, ZN)
@@ -347,7 +358,8 @@
         dyt[:, pl.ds(pl.multiple_of(s * 2 * TOK, 2 * TOK), 2 * TOK)] = grad_out.astype(BF16)
         return 0
 
-    lax.fori_loop(0, SLOTS, out_gradient, 0)
+    with jax.named_scope("out_gradient"):
+        lax.fori_loop(0, SLOTS, out_gradient, 0)
 
     low, high = pl.ds(0, HALF), pl.ds(HALF, HALF)
 
@@ -385,18 +397,13 @@
     def y_last(j):
         return remote(gall.at[far_m, j], gall.at[far_m, j], y_s.at[7, j], y_r.at[7, j], sib)
 
-    def far_halves(ref, sems):
-        return [
-            remote(ref.at[low], ref.at[low], sems[0], sems[1], up),
-            remote(ref.at[high], ref.at[high], sems[2], sems[3], up),
-        ]
-
     def stage(step, behind, run):
         j = step - behind
 
         @pl.when(jnp.logical_and(j >= 0, j < NB))
         def _():
-            run(j)
+            with jax.named_scope(run.__name__):
+                run(j)
 
     def multiply(j):
         cols = pl.ds(pl.multiple_of(j * CB, CB), CB)
@@ -450,14 +457,16 @@
 
     lax.fori_loop(0, NB + 5, pipeline_step, 0)
 
-    for i, (src, dst) in enumerate(state):
-        for copy in state_on(i, dst):
-            copy.wait_recv()
-        state_last(i, dst).start()
-    for i, (src, dst) in enumerate(state):
-        state_last(i, dst).wait_recv()
-        for copy in state_first(i, src, dst) + state_on(i, dst) + [state_last(i, dst)]:
-            copy.wait_send()
+    with jax.named_scope("state_on_wait"):
+        for i, (src, dst) in enumerate(state):
+            for copy in state_on(i, dst):
+                copy.wait_recv()
+            state_last(i, dst).start()
+    with jax.named_scope("state_last_wait"):
+        for i, (src, dst) in enumerate(state):
+            state_last(i, dst).wait_recv()
+            for copy in state_first(i, src, dst) + state_on(i, dst) + [state_last(i, dst)]:
+                copy.wait_send()
     swap.wait_send()
     for copy in inputs:
         copy.wait_send()

time: 195 us -> 195 us (level)
  no operation moved by 1% of the time
where the time goes in v2:
time: 195 us
  Pallas kernels  193 us (99%)
    pallas_call x1, Pallas kernels, gather_gradients(): pl.pallas_call(gradient_kernel, out_shape=(jax.ShapeDtypeStruct((MEMBERS,...  187 us
    pallas_call x1, Pallas kernels, update(): pl.pallas_call(update_kernel, out_shape=(jax.ShapeDtypeStruct((ROWS, COLS...  5.94 us

profile of v2, /device:TPU:1, one launch (start us, length us, event | category | flops | bytes accessed | tf_op | source)
XLA Modules:
  0.0 195.0 jit_solution(16046878266236039387)
XLA Ops:
  0.6 0.0 copy-start
  0.6 0.6 copy-done
  1.3 0.6 constant_dynamic-slice_fusion
  1.8 187.2 %shard_map.112 = (f32[8,5,160,256]{3,2,1,0:T(8,128)}, bf16[8,160,1280]{2,1,0:T(8,128)(2,1)}, f32[8,160,1280]{2,1,0:T(8,128)}, f32[8,160,1280]{2,1,0:T(8,128)}) custom-call(bf16[128,1280]{1,0:T(8,128)(2,1)} %bitcast.17, bf16[160,1280]{1,0:T(8,128)(2,1)} %bitcast.15, f32[160,1280]{1,0:T(8,128)} %bitcast.11, f32[160,1280]{1,0:T(8,128)} %bitcast.12, ...), custom_call_target="tpu_custom_call" | custom-call | flops 3355443200 | bytes 20000000 | tf_op jit(solution)/shard_map/pallas_call | solution.py:504
  189.0 5.9 %shard_map.113 = (bf16[160,1280]{1,0:T(8,128)(2,1)}, f32[160,1280]{1,0:T(8,128)}, f32[160,1280]{1,0:T(8,128)}) custom-call(s32[1]{0:T(128)} %bitcast.pick, f32[8]{0:T(128)} %rate_of.1, s32[8]{0:T(128)} %level_of.1, f32[8,5,160,256]{3,2,1,0:T(8,128)} %get-tuple-element.10.g, bf16[8,160,1280]{2,1,0:T(8,128)(2,1)} %get-tuple-element.11.w, ...), custom_call_target="tpu_custom_call" | custom-call | tf_op jit(solution)/shard_map/pallas_call | solution.py:576
Async XLA Ops:
  0.6 0.7 copy-start

commit v3 on v1

--- a/solution.py
+++ b/solution.py
@@ -19,6 +19,10 @@
 SLOTS = 8
 CB = 256
 NB = COLS // CB
+PAD = 16
+CODED = ROWS + PAD
+TOP = 32000.0
+LAG = 2
 SCALING = 1.0 / math.sqrt(HW)
 
 beta_one = 0.9
@@ -40,6 +44,20 @@
         device_id=device,
         device_id_type=MESH,
     )
+
+
+def encode(values):
+    top = jnp.max(jnp.abs(values), axis=0, keepdims=True)
+    power = jnp.clip(jnp.ceil(jnp.log2(jnp.maximum(top, 1e-30))), -100.0, 126.0)
+    codes = jnp.round(values * (TOP * jnp.exp2(-power)))
+    powers = jnp.broadcast_to(power, (PAD, values.shape[1]))
+    return jnp.concatenate([codes, powers], axis=0).astype(jnp.int32).astype(jnp.int16)
+
+
+def decode(coded):
+    wide = coded.astype(jnp.int32).astype(F32)
+    rows = wide.shape[0] - PAD
+    return wide[:rows] * (jnp.exp2(wide[rows : rows + 1]) * (1.0 / TOP))
 
 
 def gradient_kernel(
@@ -66,9 +84,13 @@
     late,
     tot,
     pbuf,
+    c1,
     r1,
+    c2,
     r2,
     rout,
+    mbuf,
+    vbuf,
     loc,
     in_s,
     in_r,
@@ -113,9 +135,13 @@
         pltpu.make_async_copy(own_rows, xbuf.at[0, 0, 0], loc.at[0]),
         pltpu.make_async_copy(w, wbuf.at[0, 0], loc.at[1]),
         pltpu.make_async_copy(tgt.at[:, xl], tbuf.at[0], loc.at[2]),
-        pltpu.make_async_copy(w, wall.at[mem], loc.at[3]),
-        pltpu.make_async_copy(m, mall.at[mem], loc.at[4]),
-        pltpu.make_async_copy(v, vall.at[mem], loc.at[5]),
+        pltpu.make_async_copy(m, mbuf, loc.at[3]),
+        pltpu.make_async_copy(v, vbuf, loc.at[4]),
+    ]
+    kept = [
+        pltpu.make_async_copy(wbuf.at[0, 0], wall.at[mem], loc.at[5]),
+        pltpu.make_async_copy(mbuf, mall.at[mem], loc.at[6]),
+        pltpu.make_async_copy(vbuf, vall.at[mem], loc.at[7]),
     ]
     for copy in locals_:
         copy.start()
@@ -198,6 +224,8 @@
         first(1, d, xbuf.at[1, 0, 0]).start()
     for copy in locals_:
         copy.wait()
+    for copy in kept:
+        copy.start()
 
     def chunks_of(s):
         one = lax.rem(zz - s + ZN, ZN)
@@ -264,6 +292,14 @@
             for copy in inputs:
                 copy.wait_recv()
 
+        @pl.when(s == SLOTS - 1)
+        def _():
+            for i, (src, dst) in enumerate(state):
+                for copy in state_first(i, src, dst):
+                    copy.wait_recv()
+                for copy in state_on(i, dst):
+                    copy.start()
+
         lax.fori_loop(done_by(s - 1) + 1, done_by(s) + 1, project_early, 0)
         return 0
 
@@ -296,12 +332,6 @@
 
     lax.fori_loop(1, ZN, send_late, 0)
     late[zz] = late_out[...]
-
-    for i, (src, dst) in enumerate(state):
-        for copy in state_first(i, src, dst):
-            copy.wait_recv()
-        for copy in state_on(i, dst):
-            copy.start()
 
     def take_early(k, total):
         src = lax.rem(zz + k, ZN)
@@ -349,18 +379,18 @@
 
     lax.fori_loop(0, SLOTS, out_gradient, 0)
 
-    low, high = pl.ds(0, HALF), pl.ds(HALF, HALF)
+    low, high = pl.ds(0, HALF), pl.ds(HALF, CODED - HALF)
 
     def hop_one(j):
         return [
-            remote(pbuf.at[j, 1, 0, low], r1.at[0, j], x_s.at[0, j], x_r.at[0, j], dev_a),
-            remote(pbuf.at[j, 1, 0, high], r1.at[1, j], x_s.at[1, j], x_r.at[1, j], dev_b),
+            remote(c1.at[0, j], r1.at[0, j], x_s.at[0, j], x_r.at[0, j], dev_a),
+            remote(c1.at[1, j], r1.at[1, j], x_s.at[1, j], x_r.at[1, j], dev_b),
         ]
 
     def hop_two(j):
         return [
-            remote(pbuf.at[j, 0, 1], r2.at[0, j], x_s.at[2, j], x_r.at[2, j], dev_a),
-            remote(pbuf.at[j, 1, 1], r2.at[1, j], x_s.at[3, j], x_r.at[3, j], dev_b),
+            remote(c2.at[0, j], r2.at[0, j], x_s.at[2, j], x_r.at[2, j], dev_a),
+            remote(c2.at[1, j], r2.at[1, j], x_s.at[3, j], x_r.at[3, j], dev_b),
         ]
 
     def y_local(j):
@@ -385,12 +415,6 @@
     def y_last(j):
         return remote(gall.at[far_m, j], gall.at[far_m, j], y_s.at[7, j], y_r.at[7, j], sib)
 
-    def far_halves(ref, sems):
-        return [
-            remote(ref.at[low], ref.at[low], sems[0], sems[1], up),
-            remote(ref.at[high], ref.at[high], sems[2], sems[3], up),
-        ]
-
     def stage(step, behind, run):
         j = step - behind
 
@@ -401,27 +425,34 @@
     def multiply(j):
         cols = pl.ds(pl.multiple_of(j * CB, CB), CB)
         for h in (1, 0):
-            part = jnp.dot(
+            part = SCALING * jnp.dot(
                 dyt[...],
                 xbuf[h, :, :, :, cols].reshape(2 * SLOTS * TOK, CB),
                 preferred_element_type=F32,
             )
-            pbuf[j, h] = (part * SCALING).reshape(2, ROWS, CB)
-        for copy in hop_one(j):
-            copy.start()
+            pbuf[j, h, 1] = part[ROWS:]
+            if h:
+                c1[0, j] = encode(part[:HALF])
+                c1[1, j] = encode(part[HALF:ROWS])
+                for copy in hop_one(j):
+                    copy.start()
+            else:
+                pbuf[j, h, 0] = part[:ROWS]
 
     def add_one(j):
         for copy in hop_one(j):
             copy.wait_recv()
-        pbuf[j, 1, 1, low] = pbuf[j, 1, 1, low] + r1[0, j]
-        pbuf[j, 0, 1, high] = pbuf[j, 0, 1, high] + r1[1, j]
+        pbuf[j, 1, 1, :HALF] = pbuf[j, 1, 1, :HALF] + decode(r1[0, j])
+        pbuf[j, 0, 1, HALF:] = pbuf[j, 0, 1, HALF:] + decode(r1[1, j])
+        c2[0, j] = encode(pbuf[j, 0, 1])
+        c2[1, j] = encode(pbuf[j, 1, 1])
         for copy in hop_two(j):
             copy.start()
 
     def add_two(j):
         for copy in hop_two(j):
             copy.wait_recv()
-        rout[j] = pbuf[j, 0, 0] + r2[0, j] + r2[1, j]
+        rout[j] = encode(pbuf[j, 0, 0] + decode(r2[0, j]) + decode(r2[1, j]))
         y_local(j).start()
         for copy in y_first(j):
             copy.start()
@@ -445,10 +476,10 @@
 
     def pipeline_step(step, _):
         for behind, run in enumerate((multiply, add_one, add_two, pass_on, pass_last, finish)):
-            stage(step, behind, run)
-        return 0
-
-    lax.fori_loop(0, NB + 5, pipeline_step, 0)
+            stage(step, LAG * behind, run)
+        return 0
+
+    lax.fori_loop(0, NB + 5 * LAG, pipeline_step, 0)
 
     for i, (src, dst) in enumerate(state):
         for copy in state_on(i, dst):
@@ -458,6 +489,8 @@
         state_last(i, dst).wait_recv()
         for copy in state_first(i, src, dst) + state_on(i, dst) + [state_last(i, dst)]:
             copy.wait_send()
+    for copy in kept:
+        copy.wait()
     swap.wait_send()
     for copy in inputs:
         copy.wait_send()
@@ -495,7 +528,7 @@
     return pl.pallas_call(
         gradient_kernel,
         out_shape=(
-            jax.ShapeDtypeStruct((MEMBERS, NB, ROWS, CB), F32),
+            jax.ShapeDtypeStruct((MEMBERS, NB, CODED, CB), jnp.int16),
             jax.ShapeDtypeStruct((MEMBERS, ROWS, COLS), BF16),
             jax.ShapeDtypeStruct((MEMBERS, ROWS, COLS), F32),
             jax.ShapeDtypeStruct((MEMBERS, ROWS, COLS), F32),
@@ -516,10 +549,14 @@
             vmem((ZN, 2, 2 * TOK), F32),
             vmem((ZN, 2 * TOK), F32),
             vmem((NB, 2, 2, ROWS, CB), F32),
-            vmem((2, NB, HALF, CB), F32),
-            vmem((2, NB, ROWS, CB), F32),
-            vmem((NB, ROWS, CB), F32),
-            dma((6,)),
+            vmem((2, NB, HALF + PAD, CB), jnp.int16),
+            vmem((2, NB, HALF + PAD, CB), jnp.int16),
+            vmem((2, NB, CODED, CB), jnp.int16),
+            vmem((2, NB, CODED, CB), jnp.int16),
+            vmem((NB, CODED, CB), jnp.int16),
+            vmem((ROWS, COLS), F32),
+            vmem((ROWS, COLS), F32),
+            dma((8,)),
             dma((5,)),
             dma((5,)),
             dma((2, 2, SLOTS)),
@@ -549,7 +586,7 @@
     p = pick[0]
     level = jnp.full((8, CB), level_of[p].astype(F32), F32)
     step_size = (rate_of[p] * 2.0 ** ((level - 4.0) / 4.0))[:1]
-    gradient = g[0, 0]
+    gradient = decode(g[0, 0])
     first = beta_one * m[0] + (1.0 - beta_one) * gradient
     second = beta_two * v[0] + (1.0 - beta_two) * gradient * gradient
     new_w[...] = (w[0].astype(F32) - step_size * first / (jnp.sqrt(second) + adam_eps)).astype(BF16)
@@ -575,7 +612,7 @@
             num_scalar_prefetch=3,
             grid=(NB,),
             in_specs=[
-                pl.BlockSpec((1, 1, ROWS, CB), lambda j, pick, rate, level: (pick[0], j, 0, 0)),
+                pl.BlockSpec((1, 1, CODED, CB), lambda j, pick, rate, level: (pick[0], j, 0, 0)),
                 pl.BlockSpec((1, ROWS, CB), member_block),
                 pl.BlockSpec((1, ROWS, CB), member_block),
                 pl.BlockSpec((1, ROWS, CB), member_block),

time: 195 us -> 132 us (0.68)
  Pallas kernels: 193 us -> 129 us
    pallas_call x1, Pallas kernels: 187 us -> 123 us  [gather_gradients(): pl.pallas_call(gradient_kernel, out_shape=(jax.ShapeDtypeStruct((MEMBERS,...]
where the time goes in v3:
time: 132 us; the launch traced here: 131 us
  Pallas kernels  129 us (98%)
    pallas_call x1, Pallas kernels, gather_gradients(): pl.pallas_call(gradient_kernel, out_shape=(jax.ShapeDtypeStruct((MEMBERS,...  123 us
    pallas_call x1, Pallas kernels, update(): pl.pallas_call(update_kernel, out_shape=(jax.ShapeDtypeStruct((ROWS, COLS...  6.04 us

profile of v3, /device:TPU:1, one launch (start us, length us, event | category | flops | bytes accessed | tf_op | source)
XLA Modules:
  0.0 131.3 jit_solution(1132259598167328248)
XLA Ops:
  0.6 0.0 copy-start
  0.6 0.6 copy-done
  1.3 0.7 constant_dynamic-slice_fusion
  1.9 123.3 %shard_map.112 = (s16[8,5,176,256]{3,2,1,0:T(8,128)(2,1)}, bf16[8,160,1280]{2,1,0:T(8,128)(2,1)}, f32[8,160,1280]{2,1,0:T(8,128)}, f32[8,160,1280]{2,1,0:T(8,128)}) custom-call(bf16[128,1280]{1,0:T(8,128)(2,1)} %bitcast.17, bf16[160,1280]{1,0:T(8,128)(2,1)} %bitcast.15, f32[160,1280]{1,0:T(8,128)} %bitcast.11, f32[160,1280]{1,0:T(8,128)} %bitcast.12, ...), custom_call_target="tpu_custom_call" | custom-call | flops 3355443200 | bytes 20000000 | tf_op jit(solution)/shard_map/pallas_call | solution.py:528
  125.3 6.0 %shard_map.113 = (bf16[160,1280]{1,0:T(8,128)(2,1)}, f32[160,1280]{1,0:T(8,128)}, f32[160,1280]{1,0:T(8,128)}) custom-call(s32[1]{0:T(128)} %bitcast.pick, f32[8]{0:T(128)} %rate_of.1, s32[8]{0:T(128)} %level_of.1, s16[8,5,176,256]{3,2,1,0:T(8,128)(2,1)} %get-tuple-element.10.g, bf16[8,160,1280]{2,1,0:T(8,128)(2,1)} %get-tuple-element.11.w, ...), custom_call_target="tpu_custom_call" | custom-call | tf_op jit(solution)/shard_map/pallas_call | solution.py:604
Async XLA Ops:
  0.6 0.7 copy-start

commit v4 on v3

--- a/solution.py
+++ b/solution.py
@@ -91,6 +91,9 @@
     rout,
     mbuf,
     vbuf,
+    mcode,
+    vcode,
+    idbuf,
     loc,
     in_s,
     in_r,
@@ -135,27 +138,26 @@
         pltpu.make_async_copy(own_rows, xbuf.at[0, 0, 0], loc.at[0]),
         pltpu.make_async_copy(w, wbuf.at[0, 0], loc.at[1]),
         pltpu.make_async_copy(tgt.at[:, xl], tbuf.at[0], loc.at[2]),
-        pltpu.make_async_copy(m, mbuf, loc.at[3]),
-        pltpu.make_async_copy(v, vbuf, loc.at[4]),
+        pltpu.make_async_copy(ids, idbuf, loc.at[3]),
+    ]
+    moments = [
+        pltpu.make_async_copy(m, mbuf, loc.at[4]),
+        pltpu.make_async_copy(v, vbuf, loc.at[5]),
     ]
     kept = [
-        pltpu.make_async_copy(wbuf.at[0, 0], wall.at[mem], loc.at[5]),
-        pltpu.make_async_copy(mbuf, mall.at[mem], loc.at[6]),
-        pltpu.make_async_copy(vbuf, vall.at[mem], loc.at[7]),
+        pltpu.make_async_copy(wbuf.at[0, 0], wall.at[mem], loc.at[6]),
+        pltpu.make_async_copy(mcode, mall.at[mem], loc.at[7]),
+        pltpu.make_async_copy(vcode, vall.at[mem], loc.at[8]),
     ]
-    for copy in locals_:
+    for copy in locals_ + moments:
         copy.start()
 
     barrier = pltpu.get_barrier_semaphore()
 
-    def greet(k, _):
-        pl.semaphore_signal(barrier, inc=1, device_id=at_z(k), device_id_type=MESH)
-        return 0
-
-    lax.fori_loop(1, ZN, greet, 0)
-    for device in (dev_a, dev_b, dev_c, up, down, sib):
+    neighbours = (right, left, dev_a, dev_b, dev_c, up, down, sib)
+    for device in neighbours:
         pl.semaphore_signal(barrier, inc=1, device_id=device, device_id_type=MESH)
-    pl.semaphore_wait(barrier, ZN - 1 + 6)
+    pl.semaphore_wait(barrier, len(neighbours))
 
     swap = remote(other_rows, xbuf.at[1, 0, 0], in_s.at[0], in_r.at[0], dev_c)
     swap.start()
@@ -186,7 +188,7 @@
     for copy in inputs:
         copy.start()
 
-    state = [(w, wall), (m, mall), (v, vall)]
+    state = [(w, wall), (mcode, mall), (vcode, vall)]
 
     def state_first(i, src, dst):
         return [
@@ -196,20 +198,24 @@
         ]
 
     def state_on(i, dst):
-        low, high = pl.ds(0, HALF), pl.ds(HALF, HALF)
+        one, two = dst.at[down_m], dst.at[up_m]
+        if i:
+            low, high = pl.ds(0, HALF), pl.ds(HALF, CODED - HALF)
+            one_low, two_high = one.at[:, low], two.at[:, high]
+        else:
+            one_low, two_high = one.at[pl.ds(0, HALF)], two.at[pl.ds(HALF, HALF)]
         return [
-            remote(dst.at[down_m, low], dst.at[down_m, low], st_s.at[i, 3], st_r.at[i, 3], up),
-            remote(dst.at[up_m, high], dst.at[up_m, high], st_s.at[i, 4], st_r.at[i, 4], down),
-            remote(dst.at[down_m], dst.at[down_m], st_s.at[i, 5], st_r.at[i, 5], sib),
-            remote(dst.at[up_m], dst.at[up_m], st_s.at[i, 6], st_r.at[i, 6], sib),
+            remote(one_low, one_low, st_s.at[i, 3], st_r.at[i, 3], up),
+            remote(two_high, two_high, st_s.at[i, 4], st_r.at[i, 4], down),
+            remote(one, one, st_s.at[i, 5], st_r.at[i, 5], sib),
+            remote(two, two, st_s.at[i, 6], st_r.at[i, 6], sib),
         ]
 
     def state_last(i, dst):
         return remote(dst.at[far_m], dst.at[far_m], st_s.at[i, 7], st_r.at[i, 7], sib)
 
-    for i, (src, dst) in enumerate(state):
-        for copy in state_first(i, src, dst):
-            copy.start()
+    for copy in state_first(0, w, wall):
+        copy.start()
 
     eye[...] = (
         lax.broadcasted_iota(jnp.int32, (ROWS, ROWS), 0)
@@ -222,6 +228,19 @@
     swap.wait_recv()
     for d in (0, 1):
         first(1, d, xbuf.at[1, 0, 0]).start()
+    for copy in moments:
+        copy.wait()
+
+    def code_moments(j, _):
+        cols = pl.ds(pl.multiple_of(j * CB, CB), CB)
+        mcode[j] = encode(mbuf[:, cols])
+        vcode[j] = encode(vbuf[:, cols])
+        return 0
+
+    lax.fori_loop(0, NB, code_moments, 0)
+    for i in (1, 2):
+        for copy in state_first(i, *state[i]):
+            copy.start()
     for copy in locals_:
         copy.wait()
     for copy in kept:
@@ -292,7 +311,7 @@
             for copy in inputs:
                 copy.wait_recv()
 
-        @pl.when(s == SLOTS - 1)
+        @pl.when(s == SLOTS - 2)
         def _():
             for i, (src, dst) in enumerate(state):
                 for copy in state_first(i, src, dst):
@@ -315,13 +334,15 @@
         early_copy(k).start()
         return 0
 
-    lax.fori_loop(1, ZN, send_early, 0)
+    lax.fori_loop(1, SLOTS, send_early, 0)
+    lax.fori_loop(SLOTS + 1, ZN, send_early, 0)
     early[zz] = stat[...]
 
     for h in (0, 1):
         remote(
             xbuf.at[h, 0, 1], xbuf.at[h, 0, 1], z_s.at[h, h, 0], z_r.at[h, h, 0], right
         ).wait_recv()
+    early_copy(SLOTS).start()
     _, _, row_one, row_two = project(0)
     late_out[pl.ds(0, 1), :] = row_one
     late_out[pl.ds(1, 1), :] = row_two
@@ -357,7 +378,7 @@
     lax.fori_loop(0, ZN, add_late, 0)
 
     def window_mask(c):
-        row = ids[pl.ds(2 * c + xl, 1), :]
+        row = idbuf[pl.ds(2 * c + xl, 1), :]
         return jnp.where(row != 0, 1.0, 0.0)
 
     def out_gradient(s, _):
@@ -475,8 +496,9 @@
             copy.wait_send()
 
     def pipeline_step(step, _):
-        for behind, run in enumerate((multiply, add_one, add_two, pass_on, pass_last, finish)):
-            stage(step, LAG * behind, run)
+        runs = (multiply, add_one, add_two, pass_on, pass_last, finish)
+        for behind in reversed(range(len(runs))):
+            stage(step, LAG * behind, runs[behind])
         return 0
 
     lax.fori_loop(0, NB + 5 * LAG, pipeline_step, 0)
@@ -530,10 +552,10 @@
         out_shape=(
             jax.ShapeDtypeStruct((MEMBERS, NB, CODED, CB), jnp.int16),
             jax.ShapeDtypeStruct((MEMBERS, ROWS, COLS), BF16),
-            jax.ShapeDtypeStruct((MEMBERS, ROWS, COLS), F32),
-            jax.ShapeDtypeStruct((MEMBERS, ROWS, COLS), F32),
+            jax.ShapeDtypeStruct((MEMBERS, NB, CODED, CB), jnp.int16),
+            jax.ShapeDtypeStruct((MEMBERS, NB, CODED, CB), jnp.int16),
         ),
-        in_specs=[anywhere] * 5 + [pl.BlockSpec(memory_space=pltpu.VMEM)],
+        in_specs=[anywhere] * 6,
         out_specs=(anywhere,) * 4,
         scratch_shapes=[
             vmem((2, SLOTS, 2, TOK, COLS), BF16),
@@ -556,7 +578,10 @@
             vmem((NB, CODED, CB), jnp.int16),
             vmem((ROWS, COLS), F32),
             vmem((ROWS, COLS), F32),
-            dma((8,)),
+            vmem((NB, CODED, CB), jnp.int16),
+            vmem((NB, CODED, CB), jnp.int16),
+            vmem((2 * ZN, 2 * TOK), jnp.int32),
+            dma((9,)),
             dma((5,)),
             dma((5,)),
             dma((2, 2, SLOTS)),
@@ -582,25 +607,57 @@
     )(ctx, w, m, v, tgt, ids)
 
 
-def update_kernel(pick, rate_of, level_of, g, w, m, v, new_w, new_m, new_v):
-    p = pick[0]
-    level = jnp.full((8, CB), level_of[p].astype(F32), F32)
-    step_size = (rate_of[p] * 2.0 ** ((level - 4.0) / 4.0))[:1]
-    gradient = decode(g[0, 0])
-    first = beta_one * m[0] + (1.0 - beta_one) * gradient
-    second = beta_two * v[0] + (1.0 - beta_two) * gradient * gradient
-    new_w[...] = (w[0].astype(F32) - step_size * first / (jnp.sqrt(second) + adam_eps)).astype(BF16)
-    new_m[...] = first
-    new_v[...] = second
-
-
-def update(pick, base_lr, perturb_index, gall, wall, mall, vall):
-    def member_block(j, pick, rate, level):
-        return (pick[0], 0, j)
-
-    def own_block(j, pick, rate, level):
-        return (0, j)
-
+def update_kernel(
+    partner, rates, levels, gall, wall, mall, vall, new_w, new_m, new_v,
+    gbuf, wbuf, mbuf, vbuf, wout, mout, vout, in_sem, out_sem,
+):
+    p = partner[lax.axis_index("member")]
+
+    def cols(j):
+        return pl.ds(j * CB, CB)
+
+    def take(j):
+        return [
+            pltpu.make_async_copy(gall.at[p, j], gbuf.at[j], in_sem.at[0, j]),
+            pltpu.make_async_copy(mall.at[p, j], mbuf.at[j], in_sem.at[1, j]),
+            pltpu.make_async_copy(vall.at[p, j], vbuf.at[j], in_sem.at[2, j]),
+            pltpu.make_async_copy(wall.at[p, :, cols(j)], wbuf.at[j], in_sem.at[3, j]),
+        ]
+
+    def give(j):
+        return [
+            pltpu.make_async_copy(mout.at[j], new_m.at[:, cols(j)], out_sem.at[0, j]),
+            pltpu.make_async_copy(vout.at[j], new_v.at[:, cols(j)], out_sem.at[1, j]),
+            pltpu.make_async_copy(wout.at[j], new_w.at[:, cols(j)], out_sem.at[2, j]),
+        ]
+
+    for j in range(NB):
+        for copy in take(j):
+            copy.start()
+    level = jnp.full((1, CB), levels[p].astype(F32), F32)
+    step_size = rates[p] * 2.0 ** ((level - 4.0) / 4.0)
+    for j in range(NB):
+        for copy in take(j):
+            copy.wait()
+        gradient = decode(gbuf[j])
+        first = beta_one * decode(mbuf[j]) + (1.0 - beta_one) * gradient
+        second = beta_two * decode(vbuf[j]) + (1.0 - beta_two) * gradient * gradient
+        mout[j] = first
+        vout[j] = second
+        wout[j] = (
+            wbuf[j].astype(F32) - step_size * first / (jnp.sqrt(second) + adam_eps)
+        ).astype(BF16)
+        for copy in give(j):
+            copy.start()
+    for j in range(NB):
+        for copy in give(j):
+            copy.wait()
+
+
+def update(partner, base_lr, perturb_index, gall, wall, mall, vall):
+    smem = pl.BlockSpec(memory_space=pltpu.SMEM)
+    anywhere = pl.BlockSpec(memory_space=pl.ANY)
+    coded = pltpu.VMEM((NB, CODED, CB), jnp.int16)
     return pl.pallas_call(
         update_kernel,
         out_shape=(
@@ -608,22 +665,21 @@
             jax.ShapeDtypeStruct((ROWS, COLS), F32),
             jax.ShapeDtypeStruct((ROWS, COLS), F32),
         ),
-        grid_spec=pltpu.PrefetchScalarGridSpec(
-            num_scalar_prefetch=3,
-            grid=(NB,),
-            in_specs=[
-                pl.BlockSpec((1, 1, CODED, CB), lambda j, pick, rate, level: (pick[0], j, 0, 0)),
-                pl.BlockSpec((1, ROWS, CB), member_block),
-                pl.BlockSpec((1, ROWS, CB), member_block),
-                pl.BlockSpec((1, ROWS, CB), member_block),
-            ],
-            out_specs=(
-                pl.BlockSpec((ROWS, CB), own_block),
-                pl.BlockSpec((ROWS, CB), own_block),
-                pl.BlockSpec((ROWS, CB), own_block),
-            ),
-        ),
-    )(pick, base_lr, perturb_index, gall, wall, mall, vall)
+        in_specs=[smem] * 3 + [anywhere] * 4,
+        out_specs=(anywhere,) * 3,
+        scratch_shapes=[
+            coded,
+            pltpu.VMEM((NB, ROWS, CB), BF16),
+            coded,
+            coded,
+            pltpu.VMEM((NB, ROWS, CB), BF16),
+            pltpu.VMEM((NB, ROWS, CB), F32),
+            pltpu.VMEM((NB, ROWS, CB), F32),
+            pltpu.SemaphoreType.DMA((4, NB)),
+            pltpu.SemaphoreType.DMA((3, NB)),
+        ],
+        compiler_params=pltpu.CompilerParams(vmem_limit_bytes=56 * 1024 * 1024),
+    )(partner, base_lr, perturb_index, gall, wall, mall, vall)
 
 
 def body(
@@ -645,8 +701,9 @@
         target[0].reshape(ZN, 2, TOK, ROWS),
         token_ids[0],
     )
-    pick = lax.dynamic_slice(partner[:, 0], (lax.axis_index("member"),), (1,))
-    new_weight, new_first, new_second = update(pick, base_lr, perturb_index, gall, wall, mall, vall)
+    new_weight, new_first, new_second = update(
+        partner.reshape(MEMBERS), base_lr, perturb_index, gall, wall, mall, vall
+    )
     return (new_weight[None], new_first[None], new_second[None])
 
 

time: 132 us -> 127 us (0.962)
  Pallas kernels: 129 us -> 126 us
    pallas_call x1, Pallas kernels: 6.04 us -> 3.56 us  [update(): pl.pallas_call(update_kernel, out_shape=(jax.ShapeDtypeStruct((ROWS, COLS...]
where the time goes in v4:
time: 127 us
  Pallas kernels  126 us (99%)
    pallas_call x1, Pallas kernels, gather_gradients(): pl.pallas_call(gradient_kernel, out_shape=(jax.ShapeDtypeStruct((MEMBERS,...  123 us
    pallas_call x1, Pallas kernels, update(): pl.pallas_call(update_kernel, out_shape=(jax.ShapeDtypeStruct((ROWS, COLS...  3.56 us

profile of v4, /device:TPU:1, one launch (start us, length us, event | category | flops | bytes accessed | tf_op | source)
XLA Modules:
  0.0 126.8 jit_solution(6460126628683463794)
XLA Ops:
  0.6 122.6 %shard_map.112 = (s16[8,5,176,256]{3,2,1,0:T(8,128)(2,1)}, bf16[8,160,1280]{2,1,0:T(8,128)(2,1)}, s16[8,5,176,256]{3,2,1,0:T(8,128)(2,1)}, s16[8,5,176,256]{3,2,1,0:T(8,128)(2,1)}) custom-call(bf16[128,1280]{1,0:T(8,128)(2,1)} %bitcast.18, bf16[160,1280]{1,0:T(8,128)(2,1)} %bitcast.16, f32[160,1280]{1,0:T(8,128)} %bitcast.12, f32[160,1280]{1,0:T(8,128)} %bitcast.13, ...), custom_call_target="tpu_custom_call" | custom-call | flops 3355443200 | bytes 20000000 | tf_op jit(solution)/shard_map/pallas_call | solution.py:550
  123.2 3.6 %shard_map.113 = (bf16[160,1280]{1,0:T(8,128)(2,1)}, f32[160,1280]{1,0:T(8,128)}, f32[160,1280]{1,0:T(8,128)}) custom-call(s32[8]{0:T(128)} %bitcast.10, f32[8]{0:T(128)} %rates.1, s32[8]{0:T(128)} %levels.1, s16[8,5,176,256]{3,2,1,0:T(8,128)(2,1)} %get-tuple-element.10.gall, bf16[8,160,1280]{2,1,0:T(8,128)(2,1)} %get-tuple-element.11.wall, ...), custom_call_target="tpu_custom_call" | custom-call | tf_op jit(solution)/shard_map/pallas_call | solution.py:661

commit v5 on v4

--- a/solution.py
+++ b/solution.py
@@ -78,11 +78,12 @@
     yt,
     gt,
     dyt,
-    stat,
-    early,
+    rows_out,
+    rows_in,
+    own_out,
+    own_in,
     late_out,
     late,
-    tot,
     pbuf,
     c1,
     r1,
@@ -101,6 +102,8 @@
     z_r,
     e_s,
     e_r,
+    o_s,
+    o_r,
     l_s,
     l_r,
     st_s,
@@ -185,8 +188,6 @@
         remote(w, wbuf.at[1, 0], in_s.at[3], in_r.at[3], dev_c),
         remote(tgt.at[:, 1 - xl], tbuf.at[1], in_s.at[4], in_r.at[4], dev_a),
     ]
-    for copy in inputs:
-        copy.start()
 
     state = [(w, wall), (mcode, mall), (vcode, vall)]
 
@@ -221,13 +222,14 @@
         lax.broadcasted_iota(jnp.int32, (ROWS, ROWS), 0)
         == lax.broadcasted_iota(jnp.int32, (ROWS, ROWS), 1)
     ).astype(BF16)
-    stat[...] = jnp.zeros_like(stat)
     lane = lax.broadcasted_iota(jnp.int32, (1, 2 * TOK), 1)
     low_lanes = lane < TOK
 
     swap.wait_recv()
     for d in (0, 1):
         first(1, d, xbuf.at[1, 0, 0]).start()
+    for copy in inputs:
+        copy.start()
     for copy in moments:
         copy.wait()
 
@@ -281,16 +283,39 @@
         crosses = jnp.sum(goal * out, axis=0, keepdims=True)
         row_one = jnp.where(low_lanes, squares, pltpu.roll(crosses, TOK, 1))
         row_two = jnp.where(low_lanes, pltpu.roll(squares, TOK, 1), crosses)
-        return one, two, row_one, row_two
+        return row_one, row_two
+
+    def row_copies(s):
+        return [
+            remote(
+                rows_out.at[2 * s + side],
+                rows_in.at[zz],
+                e_s.at[2 * s + side],
+                e_r.at[zz],
+                at_z(s if side else ZN - s),
+            )
+            for side in (0, 1)
+        ]
 
     def project_early(s, _):
-        one, two, row_one, row_two = project(s)
-        stat[pl.ds(one, 1), :] = row_one
-        stat[pl.ds(two, 1), :] = row_two
+        row_one, row_two = project(s)
+
+        @pl.when(s < SLOTS - 1)
+        def _():
+            rows_out[2 * s] = row_one
+            rows_out[2 * s + 1] = row_two
+            for copy in row_copies(s):
+                copy.start()
+
+        @pl.when(s == SLOTS - 1)
+        def _():
+            late_out[pl.ds(2, 1), :] = row_one
+            late_out[pl.ds(3, 1), :] = row_two
+
         return 0
 
     def done_by(s):
-        return jnp.minimum(jnp.maximum(2 * (s - 3), 0), SLOTS - 1)
+        return jnp.where(s < 5, 0, 2 * (s - 4) + 1)
 
     def gather_step(s, _):
         for h in (0, 1):
@@ -306,7 +331,7 @@
                     def _():
                         ring(h, s, d).start()
 
-        @pl.when(s == 4)
+        @pl.when(s == 5)
         def _():
             for copy in inputs:
                 copy.wait_recv()
@@ -324,26 +349,35 @@
 
     lax.fori_loop(1, SLOTS, gather_step, 0)
 
-    def early_copy(k):
-        return remote(stat, early.at[zz], e_s.at[k], e_r.at[zz], at_z(k))
+    def own_copy(k):
+        return remote(own_out, own_in.at[zz], o_s.at[k], o_r.at[zz], at_z(k))
 
     def late_copy(k):
         return remote(late_out, late.at[zz], l_s.at[k], l_r.at[zz], at_z(k))
 
-    def send_early(k, _):
-        early_copy(k).start()
-        return 0
-
-    lax.fori_loop(1, SLOTS, send_early, 0)
-    lax.fori_loop(SLOTS + 1, ZN, send_early, 0)
-    early[zz] = stat[...]
+    def take_row(k, total):
+        src = lax.rem(zz + k, ZN)
+        remote(own_out, rows_in.at[src], e_s.at[k], e_r.at[src], right).wait_recv()
+        return total + rows_in[src]
+
+    total = lax.fori_loop(1, SLOTS - 1, take_row, jnp.zeros((1, 2 * TOK), F32))
+    total = lax.fori_loop(SLOTS + 2, ZN, take_row, total)
+    own_out[...] = total
+    own_in[zz] = total
+
+    def send_own(k, _):
+        own_copy(k).start()
+        return 0
+
+    lax.fori_loop(1, SLOTS, send_own, 0)
+    lax.fori_loop(SLOTS + 1, ZN, send_own, 0)
 
     for h in (0, 1):
         remote(
             xbuf.at[h, 0, 1], xbuf.at[h, 0, 1], z_s.at[h, h, 0], z_r.at[h, h, 0], right
         ).wait_recv()
-    early_copy(SLOTS).start()
-    _, _, row_one, row_two = project(0)
+    own_copy(SLOTS).start()
+    row_one, row_two = project(0)
     late_out[pl.ds(0, 1), :] = row_one
     late_out[pl.ds(1, 1), :] = row_two
 
@@ -354,28 +388,19 @@
     lax.fori_loop(1, ZN, send_late, 0)
     late[zz] = late_out[...]
 
-    def take_early(k, total):
+    def take_sums(k, _):
         src = lax.rem(zz + k, ZN)
-        remote(stat, early.at[src], e_s.at[k], e_r.at[src], right).wait_recv()
-        return total + early[src]
-
-    tot[...] = lax.fori_loop(1, ZN, take_early, stat[...])
-
-    def take_late(k, _):
-        src = lax.rem(zz + k, ZN)
+        remote(own_out, own_in.at[src], o_s.at[k], o_r.at[src], right).wait_recv()
         remote(late_out, late.at[src], l_s.at[k], l_r.at[src], right).wait_recv()
         return 0
 
-    lax.fori_loop(1, ZN, take_late, 0)
-
-    def add_late(c, _):
-        opposite = lax.rem(c + SLOTS, ZN)
-        tot[pl.ds(c, 1), :] = (
-            tot[pl.ds(c, 1), :] + late[c, pl.ds(0, 1), :] + late[opposite, pl.ds(1, 1), :]
-        )
-        return 0
-
-    lax.fori_loop(0, ZN, add_late, 0)
+    lax.fori_loop(1, ZN, take_sums, 0)
+
+    def total_row(c):
+        total = own_in[c]
+        for row, behind in enumerate((0, SLOTS, SLOTS - 1, SLOTS + 1)):
+            total = total + late[lax.rem(c + behind, ZN), pl.ds(row, 1), :]
+        return total
 
     def window_mask(c):
         row = idbuf[pl.ds(2 * c + xl, 1), :]
@@ -383,7 +408,7 @@
 
     def out_gradient(s, _):
         one, two = chunks_of(s)
-        row_one, row_two = tot[pl.ds(one, 1), :], tot[pl.ds(two, 1), :]
+        row_one, row_two = total_row(one), total_row(two)
         squares = jnp.where(low_lanes, row_one, pltpu.roll(row_two, TOK, 1))
         crosses = jnp.where(low_lanes, pltpu.roll(row_one, TOK, 1), row_two)
         mask_one, mask_two = window_mask(one), window_mask(two)
@@ -392,9 +417,7 @@
         mask = jnp.where(ten == 0, first_half, second_half)
         inverse = lax.rsqrt(squares / D + norm_eps)
         projection = mask * (inverse * inverse * squares - inverse * crosses) / D
-        normed = yt[s] * inverse
-        hidden = mask * (normed - gt[s])
-        grad_out = inverse * (hidden - normed * projection)
+        grad_out = yt[s] * (inverse * inverse * (mask - projection)) - gt[s] * (inverse * mask)
         dyt[:, pl.ds(pl.multiple_of(s * 2 * TOK, 2 * TOK), 2 * TOK)] = grad_out.astype(BF16)
         return 0
 
@@ -536,11 +559,18 @@
     lax.fori_loop(1, SLOTS, drain_ring, 0)
 
     def drain_stats(k, _):
-        early_copy(k).wait_send()
+        own_copy(k).wait_send()
         late_copy(k).wait_send()
         return 0
 
     lax.fori_loop(1, ZN, drain_stats, 0)
+
+    def drain_rows(s, _):
+        for copy in row_copies(s):
+            copy.wait_send()
+        return 0
+
+    lax.fori_loop(1, SLOTS - 1, drain_rows, 0)
 
 
 def gather_gradients(ctx, w, m, v, tgt, ids):
@@ -565,11 +595,12 @@
             vmem((SLOTS, 2 * ROWS, 2 * TOK), F32),
             vmem((SLOTS, 2 * ROWS, 2 * TOK), F32),
             vmem((2 * ROWS, SLOTS * 2 * TOK), BF16),
-            vmem((ZN, 2 * TOK), F32),
-            vmem((ZN, ZN, 2 * TOK), F32),
-            vmem((2, 2 * TOK), F32),
-            vmem((ZN, 2, 2 * TOK), F32),
-            vmem((ZN, 2 * TOK), F32),
+            vmem((2 * SLOTS, 1, 2 * TOK), F32),
+            vmem((ZN, 1, 2 * TOK), F32),
+            vmem((1, 2 * TOK), F32),
+            vmem((ZN, 1, 2 * TOK), F32),
+            vmem((4, 2 * TOK), F32),
+            vmem((ZN, 4, 2 * TOK), F32),
             vmem((NB, 2, 2, ROWS, CB), F32),
             vmem((2, NB, HALF + PAD, CB), jnp.int16),
             vmem((2, NB, HALF + PAD, CB), jnp.int16),
@@ -586,6 +617,8 @@
             dma((5,)),
             dma((2, 2, SLOTS)),
             dma((2, 2, SLOTS)),
+            dma((ZN,)),
+            dma((ZN,)),
             dma((ZN,)),
             dma((ZN,)),
             dma((ZN,)),

time: 127 us -> 125 us (0.984)
  Pallas kernels: 126 us -> 124 us
    pallas_call x1, Pallas kernels: 123 us -> 121 us  [gather_gradients(): pl.pallas_call(gradient_kernel, out_shape=(jax.ShapeDtypeStruct((MEMBERS,...]
where the time goes in v5:
time: 125 us
  Pallas kernels  124 us (99%)
    pallas_call x1, Pallas kernels, gather_gradients(): pl.pallas_call(gradient_kernel, out_shape=(jax.ShapeDtypeStruct((MEMBERS,...  121 us
    pallas_call x1, Pallas kernels, update(): pl.pallas_call(update_kernel, out_shape=(jax.ShapeDtypeStruct((ROWS, COLS...  3.56 us

profile of v5, /device:TPU:1, one launch (start us, length us, event | category | flops | bytes accessed | tf_op | source)
XLA Modules:
  0.0 125.0 jit_solution(152453263839584881)
XLA Ops:
  0.6 120.9 %shard_map.112 = (s16[8,5,176,256]{3,2,1,0:T(8,128)(2,1)}, bf16[8,160,1280]{2,1,0:T(8,128)(2,1)}, s16[8,5,176,256]{3,2,1,0:T(8,128)(2,1)}, s16[8,5,176,256]{3,2,1,0:T(8,128)(2,1)}) custom-call(bf16[128,1280]{1,0:T(8,128)(2,1)} %bitcast.18, bf16[160,1280]{1,0:T(8,128)(2,1)} %bitcast.16, f32[160,1280]{1,0:T(8,128)} %bitcast.12, f32[160,1280]{1,0:T(8,128)} %bitcast.13, ...), custom_call_target="tpu_custom_call" | custom-call | flops 3355443200 | bytes 20000000 | tf_op jit(solution)/shard_map/pallas_call | solution.py:580
  121.5 3.6 %shard_map.113 = (bf16[160,1280]{1,0:T(8,128)(2,1)}, f32[160,1280]{1,0:T(8,128)}, f32[160,1280]{1,0:T(8,128)}) custom-call(s32[8]{0:T(128)} %bitcast.10, f32[8]{0:T(128)} %rates.1, s32[8]{0:T(128)} %levels.1, s16[8,5,176,256]{3,2,1,0:T(8,128)(2,1)} %get-tuple-element.10.gall, bf16[8,160,1280]{2,1,0:T(8,128)(2,1)} %get-tuple-element.11.wall, ...), custom_call_target="tpu_custom_call" | custom-call | tf_op jit(solution)/shard_map/pallas_call | solution.py:694

commit v6 on v5

--- a/solution.py
+++ b/solution.py
@@ -388,6 +388,41 @@
     lax.fori_loop(1, ZN, send_late, 0)
     late[zz] = late_out[...]
 
+    for i, (src, dst) in enumerate(state):
+        for copy in state_on(i, dst):
+            copy.wait_recv()
+        state_last(i, dst).start()
+    for copy in kept:
+        copy.wait()
+    swap.wait_send()
+    for copy in inputs:
+        copy.wait_send()
+    for d in (0, 1):
+        first(0, d, own_rows).wait_send()
+        first(1, d, xbuf.at[1, 0, 0]).wait_send()
+
+    def drain_ring(s, _):
+        for h in (0, 1):
+            for d in (0, 1):
+                if d == h:
+                    ring(h, s, d).wait_send()
+                else:
+
+                    @pl.when(s < SLOTS - 1)
+                    def _():
+                        ring(h, s, d).wait_send()
+
+        return 0
+
+    lax.fori_loop(1, SLOTS, drain_ring, 0)
+
+    def drain_rows(s, _):
+        for copy in row_copies(s):
+            copy.wait_send()
+        return 0
+
+    lax.fori_loop(1, SLOTS - 1, drain_rows, 0)
+
     def take_sums(k, _):
         src = lax.rem(zz + k, ZN)
         remote(own_out, own_in.at[src], o_s.at[k], o_r.at[src], right).wait_recv()
@@ -518,59 +553,27 @@
         for copy in hop_one(j) + hop_two(j) + y_first(j) + y_on(j) + [y_last(j)]:
             copy.wait_send()
 
+    def drain_stats(k, _):
+        own_copy(k).wait_send()
+        late_copy(k).wait_send()
+        return 0
+
     def pipeline_step(step, _):
         runs = (multiply, add_one, add_two, pass_on, pass_last, finish)
         for behind in reversed(range(len(runs))):
             stage(step, LAG * behind, runs[behind])
+
+        @pl.when(step == NB)
+        def _():
+            lax.fori_loop(1, ZN, drain_stats, 0)
+            for i, (src, dst) in enumerate(state):
+                state_last(i, dst).wait_recv()
+                for copy in state_first(i, src, dst) + state_on(i, dst) + [state_last(i, dst)]:
+                    copy.wait_send()
+
         return 0
 
     lax.fori_loop(0, NB + 5 * LAG, pipeline_step, 0)
-
-    for i, (src, dst) in enumerate(state):
-        for copy in state_on(i, dst):
-            copy.wait_recv()
-        state_last(i, dst).start()
-    for i, (src, dst) in enumerate(state):
-        state_last(i, dst).wait_recv()
-        for copy in state_first(i, src, dst) + state_on(i, dst) + [state_last(i, dst)]:
-            copy.wait_send()
-    for copy in kept:
-        copy.wait()
-    swap.wait_send()
-    for copy in inputs:
-        copy.wait_send()
-    for d in (0, 1):
-        first(0, d, own_rows).wait_send()
-        first(1, d, xbuf.at[1, 0, 0]).wait_send()
-
-    def drain_ring(s, _):
-        for h in (0, 1):
-            for d in (0, 1):
-                if d == h:
-                    ring(h, s, d).wait_send()
-                else:
-
-                    @pl.when(s < SLOTS - 1)
-                    def _():
-                        ring(h, s, d).wait_send()
-
-        return 0
-
-    lax.fori_loop(1, SLOTS, drain_ring, 0)
-
-    def drain_stats(k, _):
-        own_copy(k).wait_send()
-        late_copy(k).wait_send()
-        return 0
-
-    lax.fori_loop(1, ZN, drain_stats, 0)
-
-    def drain_rows(s, _):
-        for copy in row_copies(s):
-            copy.wait_send()
-        return 0
-
-    lax.fori_loop(1, SLOTS - 1, drain_rows, 0)
 
 
 def gather_gradients(ctx, w, m, v, tgt, ids):

time: 125 us -> 122 us (0.976)
  Pallas kernels: 124 us -> 121 us
    pallas_call x1, Pallas kernels: 121 us -> 118 us  [gather_gradients(): pl.pallas_call(gradient_kernel, out_shape=(jax.ShapeDtypeStruct((MEMBERS,...]
where the time goes in v6:
time: 122 us
  Pallas kernels  121 us (99%)
    pallas_call x1, Pallas kernels, gather_gradients(): pl.pallas_call(gradient_kernel, out_shape=(jax.ShapeDtypeStruct((MEMBERS,...  118 us
    pallas_call x1, Pallas kernels, update(): pl.pallas_call(update_kernel, out_shape=(jax.ShapeDtypeStruct((ROWS, COLS...  3.56 us

profile of v6, /device:TPU:1, one launch (start us, length us, event | category | flops | bytes accessed | tf_op | source)
XLA Modules:
  0.0 121.8 jit_solution(8699997542423570213)
XLA Ops:
  0.6 117.6 %shard_map.112 = (s16[8,5,176,256]{3,2,1,0:T(8,128)(2,1)}, bf16[8,160,1280]{2,1,0:T(8,128)(2,1)}, s16[8,5,176,256]{3,2,1,0:T(8,128)(2,1)}, s16[8,5,176,256]{3,2,1,0:T(8,128)(2,1)}) custom-call(bf16[128,1280]{1,0:T(8,128)(2,1)} %bitcast.18, bf16[160,1280]{1,0:T(8,128)(2,1)} %bitcast.16, f32[160,1280]{1,0:T(8,128)} %bitcast.12, f32[160,1280]{1,0:T(8,128)} %bitcast.13, ...), custom_call_target="tpu_custom_call" | custom-call | flops 3355443200 | bytes 20000000 | tf_op jit(solution)/shard_map/pallas_call | solution.py:583
  118.2 3.6 %shard_map.113 = (bf16[160,1280]{1,0:T(8,128)(2,1)}, f32[160,1280]{1,0:T(8,128)}, f32[160,1280]{1,0:T(8,128)}) custom-call(s32[8]{0:T(128)} %bitcast.10, f32[8]{0:T(128)} %rates.1, s32[8]{0:T(128)} %levels.1, s16[8,5,176,256]{3,2,1,0:T(8,128)(2,1)} %get-tuple-element.10.gall, bf16[8,160,1280]{2,1,0:T(8,128)(2,1)} %get-tuple-element.11.wall, ...), custom_call_target="tpu_custom_call" | custom-call | tf_op jit(solution)/shard_map/pallas_call | solution.py:697

commit v7 on v6

--- a/solution.py
+++ b/solution.py
@@ -17,8 +17,10 @@
 HALF = 80
 TOK = 64
 SLOTS = 8
-CB = 256
-NB = COLS // CB
+CB = 128
+NP = COLS // CB
+NB = 6
+PART = 32
 PAD = 16
 CODED = ROWS + PAD
 TOP = 32000.0
@@ -162,31 +164,55 @@
         pl.semaphore_signal(barrier, inc=1, device_id=device, device_id_type=MESH)
     pl.semaphore_wait(barrier, len(neighbours))
 
-    swap = remote(other_rows, xbuf.at[1, 0, 0], in_s.at[0], in_r.at[0], dev_c)
-    swap.start()
-
-    def ring(h, s, d):
-        dst = xbuf.at[h, lax.rem(s + 1, SLOTS), d if d else s // (SLOTS - 1)]
+    swaps = [
+        remote(
+            other_rows.at[pl.ds(part * PART, PART)],
+            xbuf.at[1, 0, 0, pl.ds(part * PART, PART)],
+            in_s.at[4 + part],
+            in_r.at[4 + part],
+            dev_c,
+        )
+        for part in range(TOK // PART)
+    ]
+    for copy in swaps:
+        copy.start()
+
+    messages = [(h, part) for h in (0, 1) for part in range(TOK // PART)]
+
+    def rows_of(part):
+        return pl.ds(part * PART, PART)
+
+    def ring(h, part, s, d):
+        dst = xbuf.at[h, lax.rem(s + 1, SLOTS), d if d else s // (SLOTS - 1), rows_of(part)]
         return remote(
-            xbuf.at[h, s, d],
+            xbuf.at[h, s, d, rows_of(part)],
             dst,
-            z_s.at[d, h, s],
-            z_r.at[d, h, lax.rem(s + 1, SLOTS)],
+            z_s.at[d, h, part, s],
+            z_r.at[d, h, part, lax.rem(s + 1, SLOTS)],
             left if d else right,
         )
 
-    def first(h, d, src):
+    def arrived(h, part, s, d):
+        dst = xbuf.at[h, s, d, rows_of(part)]
+        remote(dst, dst, z_s.at[d, h, part, s], z_r.at[d, h, part, s], right).wait_recv()
+
+    def first(h, part, d, src):
         return remote(
-            src, xbuf.at[h, 1, d], z_s.at[d, h, 0], z_r.at[d, h, 1], left if d else right
+            src.at[rows_of(part)],
+            xbuf.at[h, 1, d, rows_of(part)],
+            z_s.at[d, h, part, 0],
+            z_r.at[d, h, part, 1],
+            left if d else right,
         )
 
-    for d in (0, 1):
-        first(0, d, own_rows).start()
+    for part in range(TOK // PART):
+        for d in (0, 1):
+            first(0, part, d, own_rows).start()
     inputs = [
         remote(w, wbuf.at[0, 1], in_s.at[1], in_r.at[1], dev_a),
         remote(w, wbuf.at[1, 1], in_s.at[2], in_r.at[2], dev_b),
         remote(w, wbuf.at[1, 0], in_s.at[3], in_r.at[3], dev_c),
-        remote(tgt.at[:, 1 - xl], tbuf.at[1], in_s.at[4], in_r.at[4], dev_a),
+        remote(tgt.at[:, 1 - xl], tbuf.at[1], in_s.at[0], in_r.at[0], dev_a),
     ]
 
     state = [(w, wall), (mcode, mall), (vcode, vall)]
@@ -225,9 +251,10 @@
     lane = lax.broadcasted_iota(jnp.int32, (1, 2 * TOK), 1)
     low_lanes = lane < TOK
 
-    swap.wait_recv()
-    for d in (0, 1):
-        first(1, d, xbuf.at[1, 0, 0]).start()
+    for part, swap in enumerate(swaps):
+        swap.wait_recv()
+        for d in (0, 1):
+            first(1, part, d, xbuf.at[1, 0, 0]).start()
     for copy in inputs:
         copy.start()
     for copy in moments:
@@ -239,7 +266,7 @@
         vcode[j] = encode(vbuf[:, cols])
         return 0
 
-    lax.fori_loop(0, NB, code_moments, 0)
+    lax.fori_loop(0, NP, code_moments, 0)
     for i in (1, 2):
         for copy in state_first(i, *state[i]):
             copy.start()
@@ -318,18 +345,16 @@
         return jnp.where(s < 5, 0, 2 * (s - 4) + 1)
 
     def gather_step(s, _):
-        for h in (0, 1):
+        for h, part in messages:
             for d in (0, 1):
-                remote(
-                    xbuf.at[h, s, d], xbuf.at[h, s, d], z_s.at[d, h, s], z_r.at[d, h, s], right
-                ).wait_recv()
+                arrived(h, part, s, d)
                 if d == h:
-                    ring(h, s, d).start()
+                    ring(h, part, s, d).start()
                 else:
 
                     @pl.when(s < SLOTS - 1)
                     def _():
-                        ring(h, s, d).start()
+                        ring(h, part, s, d).start()
 
         @pl.when(s == 5)
         def _():
@@ -372,10 +397,9 @@
     lax.fori_loop(1, SLOTS, send_own, 0)
     lax.fori_loop(SLOTS + 1, ZN, send_own, 0)
 
-    for h in (0, 1):
-        remote(
-            xbuf.at[h, 0, 1], xbuf.at[h, 0, 1], z_s.at[h, h, 0], z_r.at[h, h, 0], right
-        ).wait_recv()
+    for h, part in messages:
+        dst = xbuf.at[h, 0, 1, rows_of(part)]
+        remote(dst, dst, z_s.at[h, h, part, 0], z_r.at[h, h, part, 0], right).wait_recv()
     own_copy(SLOTS).start()
     row_one, row_two = project(0)
     late_out[pl.ds(0, 1), :] = row_one
@@ -394,23 +418,23 @@
         state_last(i, dst).start()
     for copy in kept:
         copy.wait()
-    swap.wait_send()
-    for copy in inputs:
+    for copy in inputs + swaps:
         copy.wait_send()
-    for d in (0, 1):
-        first(0, d, own_rows).wait_send()
-        first(1, d, xbuf.at[1, 0, 0]).wait_send()
+    for part in range(TOK // PART):
+        for d in (0, 1):
+            first(0, part, d, own_rows).wait_send()
+            first(1, part, d, xbuf.at[1, 0, 0]).wait_send()
 
     def drain_ring(s, _):
-        for h in (0, 1):
+        for h, part in messages:
             for d in (0, 1):
                 if d == h:
-                    ring(h, s, d).wait_send()
+                    ring(h, part, s, d).wait_send()
                 else:
 
                     @pl.when(s < SLOTS - 1)
                     def _():
-                        ring(h, s, d).wait_send()
+                        ring(h, part, s, d).wait_send()
 
         return 0
 
@@ -460,97 +484,120 @@
 
     low, high = pl.ds(0, HALF), pl.ds(HALF, CODED - HALF)
 
-    def hop_one(j):
+    def pieces(j, n):
+        return pl.ds(jnp.maximum(2 * j - 1, 0), n)
+
+    def hop_one(j, n):
+        at = pieces(j, n)
         return [
-            remote(c1.at[0, j], r1.at[0, j], x_s.at[0, j], x_r.at[0, j], dev_a),
-            remote(c1.at[1, j], r1.at[1, j], x_s.at[1, j], x_r.at[1, j], dev_b),
+            remote(c1.at[0, at], r1.at[0, at], x_s.at[0, j], x_r.at[0, j], dev_a),
+            remote(c1.at[1, at], r1.at[1, at], x_s.at[1, j], x_r.at[1, j], dev_b),
         ]
 
-    def hop_two(j):
+    def hop_two(j, n):
+        at = pieces(j, n)
         return [
-            remote(c2.at[0, j], r2.at[0, j], x_s.at[2, j], x_r.at[2, j], dev_a),
-            remote(c2.at[1, j], r2.at[1, j], x_s.at[3, j], x_r.at[3, j], dev_b),
+            remote(c2.at[0, at], r2.at[0, at], x_s.at[2, j], x_r.at[2, j], dev_a),
+            remote(c2.at[1, at], r2.at[1, at], x_s.at[3, j], x_r.at[3, j], dev_b),
         ]
 
-    def y_local(j):
-        return pltpu.make_async_copy(rout.at[j], gall.at[mem, j], y_l.at[j])
-
-    def y_first(j):
+    def y_local(j, n):
+        at = pieces(j, n)
+        return pltpu.make_async_copy(rout.at[at], gall.at[mem, at], y_l.at[j])
+
+    def y_first(j, n):
+        at = pieces(j, n)
         return [
-            remote(rout.at[j], gall.at[mem, j], y_s.at[0, j], y_r.at[0, j], up),
-            remote(rout.at[j], gall.at[mem, j], y_s.at[1, j], y_r.at[1, j], down),
-            remote(rout.at[j], gall.at[mem, j], y_s.at[2, j], y_r.at[2, j], sib),
+            remote(rout.at[at], gall.at[mem, at], y_s.at[0, j], y_r.at[0, j], up),
+            remote(rout.at[at], gall.at[mem, at], y_s.at[1, j], y_r.at[1, j], down),
+            remote(rout.at[at], gall.at[mem, at], y_s.at[2, j], y_r.at[2, j], sib),
         ]
 
-    def y_on(j):
-        one, two = gall.at[down_m, j], gall.at[up_m, j]
+    def y_on(j, n):
+        at = pieces(j, n)
+        one, two = gall.at[down_m, at], gall.at[up_m, at]
         return [
-            remote(one.at[low], one.at[low], y_s.at[3, j], y_r.at[3, j], up),
-            remote(two.at[high], two.at[high], y_s.at[4, j], y_r.at[4, j], down),
+            remote(one.at[:, low], one.at[:, low], y_s.at[3, j], y_r.at[3, j], up),
+            remote(two.at[:, high], two.at[:, high], y_s.at[4, j], y_r.at[4, j], down),
             remote(one, one, y_s.at[5, j], y_r.at[5, j], sib),
             remote(two, two, y_s.at[6, j], y_r.at[6, j], sib),
         ]
 
-    def y_last(j):
-        return remote(gall.at[far_m, j], gall.at[far_m, j], y_s.at[7, j], y_r.at[7, j], sib)
+    def y_last(j, n):
+        far = gall.at[far_m, pieces(j, n)]
+        return remote(far, far, y_s.at[7, j], y_r.at[7, j], sib)
 
     def stage(step, behind, run):
         j = step - behind
 
-        @pl.when(jnp.logical_and(j >= 0, j < NB))
+        @pl.when(jnp.logical_or(j == 0, j == NB - 1))
         def _():
-            run(j)
-
-    def multiply(j):
-        cols = pl.ds(pl.multiple_of(j * CB, CB), CB)
+            run(j, 1)
+
+        @pl.when(jnp.logical_and(j > 0, j < NB - 1))
+        def _():
+            run(j, 2)
+
+    def multiply(j, n):
+        at = jnp.maximum(2 * j - 1, 0)
+        cols = pl.ds(pl.multiple_of(at * CB, CB), n * CB)
         for h in (1, 0):
-            part = SCALING * jnp.dot(
+            block = SCALING * jnp.dot(
                 dyt[...],
-                xbuf[h, :, :, :, cols].reshape(2 * SLOTS * TOK, CB),
+                xbuf[h, :, :, :, cols].reshape(2 * SLOTS * TOK, n * CB),
                 preferred_element_type=F32,
             )
-            pbuf[j, h, 1] = part[ROWS:]
+            for i in range(n):
+                part = block[:, i * CB : (i + 1) * CB]
+                pbuf[at + i, h, 1] = part[ROWS:]
+                if h:
+                    c1[0, at + i] = encode(part[:HALF])
+                    c1[1, at + i] = encode(part[HALF:ROWS])
+                else:
+                    pbuf[at + i, h, 0] = part[:ROWS]
             if h:
-                c1[0, j] = encode(part[:HALF])
-                c1[1, j] = encode(part[HALF:ROWS])
-                for copy in hop_one(j):
+                for copy in hop_one(j, n):
                     copy.start()
-            else:
-                pbuf[j, h, 0] = part[:ROWS]
-
-    def add_one(j):
-        for copy in hop_one(j):
+
+    def add_one(j, n):
+        for copy in hop_one(j, n):
             copy.wait_recv()
-        pbuf[j, 1, 1, :HALF] = pbuf[j, 1, 1, :HALF] + decode(r1[0, j])
-        pbuf[j, 0, 1, HALF:] = pbuf[j, 0, 1, HALF:] + decode(r1[1, j])
-        c2[0, j] = encode(pbuf[j, 0, 1])
-        c2[1, j] = encode(pbuf[j, 1, 1])
-        for copy in hop_two(j):
+        for i in range(n):
+            k = jnp.maximum(2 * j - 1, 0) + i
+            pbuf[k, 1, 1, :HALF] = pbuf[k, 1, 1, :HALF] + decode(r1[0, k])
+            pbuf[k, 0, 1, HALF:] = pbuf[k, 0, 1, HALF:] + decode(r1[1, k])
+            c2[0, k] = encode(pbuf[k, 0, 1])
+            c2[1, k] = encode(pbuf[k, 1, 1])
+        for copy in hop_two(j, n):
             copy.start()
 
-    def add_two(j):
-        for copy in hop_two(j):
+    def add_two(j, n):
+        for copy in hop_two(j, n):
             copy.wait_recv()
-        rout[j] = encode(pbuf[j, 0, 0] + decode(r2[0, j]) + decode(r2[1, j]))
-        y_local(j).start()
-        for copy in y_first(j):
+        for i in range(n):
+            k = jnp.maximum(2 * j - 1, 0) + i
+            rout[k] = encode(pbuf[k, 0, 0] + decode(r2[0, k]) + decode(r2[1, k]))
+        y_local(j, n).start()
+        for copy in y_first(j, n):
             copy.start()
 
-    def pass_on(j):
-        for copy in y_first(j):
+    def pass_on(j, n):
+        for copy in y_first(j, n):
             copy.wait_recv()
-        for copy in y_on(j):
+        for copy in y_on(j, n):
             copy.start()
 
-    def pass_last(j):
-        for copy in y_on(j):
+    def pass_last(j, n):
+        for copy in y_on(j, n):
             copy.wait_recv()
-        y_last(j).start()
-
-    def finish(j):
-        y_last(j).wait_recv()
-        y_local(j).wait()
-        for copy in hop_one(j) + hop_two(j) + y_first(j) + y_on(j) + [y_last(j)]:
+        y_last(j, n).start()
+
+    def finish(j, n):
+        y_last(j, n).wait_recv()
+        y_local(j, n).wait()
+        for copy in (
+            hop_one(j, n) + hop_two(j, n) + y_first(j, n) + y_on(j, n) + [y_last(j, n)]
+        ):
             copy.wait_send()
 
     def drain_stats(k, _):
@@ -583,10 +630,10 @@
     return pl.pallas_call(
         gradient_kernel,
         out_shape=(
-            jax.ShapeDtypeStruct((MEMBERS, NB, CODED, CB), jnp.int16),
+            jax.ShapeDtypeStruct((MEMBERS, NP, CODED, CB), jnp.int16),
             jax.ShapeDtypeStruct((MEMBERS, ROWS, COLS), BF16),
-            jax.ShapeDtypeStruct((MEMBERS, NB, CODED, CB), jnp.int16),
-            jax.ShapeDtypeStruct((MEMBERS, NB, CODED, CB), jnp.int16),
+            jax.ShapeDtypeStruct((MEMBERS, NP, CODED, CB), jnp.int16),
+            jax.ShapeDtypeStruct((MEMBERS, NP, CODED, CB), jnp.int16),
         ),
         in_specs=[anywhere] * 6,
         out_specs=(anywhere,) * 4,
@@ -604,22 +651,22 @@
             vmem((ZN, 1, 2 * TOK), F32),
             vmem((4, 2 * TOK), F32),
             vmem((ZN, 4, 2 * TOK), F32),
-            vmem((NB, 2, 2, ROWS, CB), F32),
-            vmem((2, NB, HALF + PAD, CB), jnp.int16),
-            vmem((2, NB, HALF + PAD, CB), jnp.int16),
-            vmem((2, NB, CODED, CB), jnp.int16),
-            vmem((2, NB, CODED, CB), jnp.int16),
-            vmem((NB, CODED, CB), jnp.int16),
+            vmem((NP, 2, 2, ROWS, CB), F32),
+            vmem((2, NP, HALF + PAD, CB), jnp.int16),
+            vmem((2, NP, HALF + PAD, CB), jnp.int16),
+            vmem((2, NP, CODED, CB), jnp.int16),
+            vmem((2, NP, CODED, CB), jnp.int16),
+            vmem((NP, CODED, CB), jnp.int16),
             vmem((ROWS, COLS), F32),
             vmem((ROWS, COLS), F32),
-            vmem((NB, CODED, CB), jnp.int16),
-            vmem((NB, CODED, CB), jnp.int16),
+            vmem((NP, CODED, CB), jnp.int16),
+            vmem((NP, CODED, CB), jnp.int16),
             vmem((2 * ZN, 2 * TOK), jnp.int32),
             dma((9,)),
-            dma((5,)),
-            dma((5,)),
-            dma((2, 2, SLOTS)),
-            dma((2, 2, SLOTS)),
+            dma((6,)),
+            dma((6,)),
+            dma((2, 2, TOK // PART, SLOTS)),
+            dma((2, 2, TOK // PART, SLOTS)),
             dma((ZN,)),
             dma((ZN,)),
             dma((ZN,)),
@@ -650,13 +697,16 @@
     p = partner[lax.axis_index("member")]
 
     def cols(j):
-        return pl.ds(j * CB, CB)
+        return pl.ds(j * 2 * CB, 2 * CB)
+
+    def pair(j):
+        return pl.ds(2 * j, 2)
 
     def take(j):
         return [
-            pltpu.make_async_copy(gall.at[p, j], gbuf.at[j], in_sem.at[0, j]),
-            pltpu.make_async_copy(mall.at[p, j], mbuf.at[j], in_sem.at[1, j]),
-            pltpu.make_async_copy(vall.at[p, j], vbuf.at[j], in_sem.at[2, j]),
+            pltpu.make_async_copy(gall.at[p, pair(j)], gbuf.at[pair(j)], in_sem.at[0, j]),
+            pltpu.make_async_copy(mall.at[p, pair(j)], mbuf.at[pair(j)], in_sem.at[1, j]),
+            pltpu.make_async_copy(vall.at[p, pair(j)], vbuf.at[pair(j)], in_sem.at[2, j]),
             pltpu.make_async_copy(wall.at[p, :, cols(j)], wbuf.at[j], in_sem.at[3, j]),
         ]
 
@@ -667,25 +717,27 @@
             pltpu.make_async_copy(wout.at[j], new_w.at[:, cols(j)], out_sem.at[2, j]),
         ]
 
-    for j in range(NB):
+    for j in range(NP // 2):
         for copy in take(j):
             copy.start()
     level = jnp.full((1, CB), levels[p].astype(F32), F32)
     step_size = rates[p] * 2.0 ** ((level - 4.0) / 4.0)
-    for j in range(NB):
+    for j in range(NP // 2):
         for copy in take(j):
             copy.wait()
-        gradient = decode(gbuf[j])
-        first = beta_one * decode(mbuf[j]) + (1.0 - beta_one) * gradient
-        second = beta_two * decode(vbuf[j]) + (1.0 - beta_two) * gradient * gradient
-        mout[j] = first
-        vout[j] = second
-        wout[j] = (
-            wbuf[j].astype(F32) - step_size * first / (jnp.sqrt(second) + adam_eps)
-        ).astype(BF16)
+        for i in range(2):
+            k, at = 2 * j + i, slice(i * CB, (i + 1) * CB)
+            gradient = decode(gbuf[k])
+            first = beta_one * decode(mbuf[k]) + (1.0 - beta_one) * gradient
+            second = beta_two * decode(vbuf[k]) + (1.0 - beta_two) * gradient * gradient
+            mout[j, :, at] = first
+            vout[j, :, at] = second
+            wout[j, :, at] = (
+                wbuf[j, :, at].astype(F32) - step_size * first / (jnp.sqrt(second) + adam_eps)
+            ).astype(BF16)
         for copy in give(j):
             copy.start()
-    for j in range(NB):
+    for j in range(NP // 2):
         for copy in give(j):
             copy.wait()
 
@@ -693,7 +745,7 @@
 def update(partner, base_lr, perturb_index, gall, wall, mall, vall):
     smem = pl.BlockSpec(memory_space=pltpu.SMEM)
     anywhere = pl.BlockSpec(memory_space=pl.ANY)
-    coded = pltpu.VMEM((NB, CODED, CB), jnp.int16)
+    coded = pltpu.VMEM((NP, CODED, CB), jnp.int16)
     return pl.pallas_call(
         update_kernel,
         out_shape=(
@@ -705,14 +757,14 @@
         out_specs=(anywhere,) * 3,
         scratch_shapes=[
             coded,
-            pltpu.VMEM((NB, ROWS, CB), BF16),
+            pltpu.VMEM((NP // 2, ROWS, 2 * CB), BF16),
             coded,
             coded,
-            pltpu.VMEM((NB, ROWS, CB), BF16),
-            pltpu.VMEM((NB, ROWS, CB), F32),
-            pltpu.VMEM((NB, ROWS, CB), F32),
-            pltpu.SemaphoreType.DMA((4, NB)),
-            pltpu.SemaphoreType.DMA((3, NB)),
+            pltpu.VMEM((NP // 2, ROWS, 2 * CB), BF16),
+            pltpu.VMEM((NP // 2, ROWS, 2 * CB), F32),
+            pltpu.VMEM((NP // 2, ROWS, 2 * CB), F32),
+            pltpu.SemaphoreType.DMA((4, NP // 2)),
+            pltpu.SemaphoreType.DMA((3, NP // 2)),
         ],
         compiler_params=pltpu.CompilerParams(vmem_limit_bytes=56 * 1024 * 1024),
     )(partner, base_lr, perturb_index, gall, wall, mall, vall)

time: 122 us -> 123 us (level)
  no operation moved by 1% of the time
where the time goes in v7:
time: 123 us; the launch traced here: 122 us
  Pallas kernels  122 us (99%)
    pallas_call x1, Pallas kernels, gather_gradients(): pl.pallas_call(gradient_kernel, out_shape=(jax.ShapeDtypeStruct((MEMBERS,...  118 us
    pallas_call x1, Pallas kernels, update(): pl.pallas_call(update_kernel, out_shape=(jax.ShapeDtypeStruct((ROWS, COLS...  3.58 us

profile of v7, /device:TPU:1, one launch (start us, length us, event | category | flops | bytes accessed | tf_op | source)
XLA Modules:
  0.0 122.5 jit_solution(15060347844577404069)
XLA Ops:
  0.6 118.3 %shard_map.112 = (s16[8,10,176,128]{3,2,1,0:T(8,128)(2,1)}, bf16[8,160,1280]{2,1,0:T(8,128)(2,1)}, s16[8,10,176,128]{3,2,1,0:T(8,128)(2,1)}, s16[8,10,176,128]{3,2,1,0:T(8,128)(2,1)}) custom-call(bf16[128,1280]{1,0:T(8,128)(2,1)} %bitcast.18, bf16[160,1280]{1,0:T(8,128)(2,1)} %bitcast.16, f32[160,1280]{1,0:T(8,128)} %bitcast.12, f32[160,1280]{1,0:T(8,128)} %bitcast.13, ...), custom_call_target="tpu_custom_call" | custom-call | flops 3355443200 | bytes 20000000 | tf_op jit(solution)/shard_map/pallas_call | solution.py:630
  118.9 3.6 %shard_map.113 = (bf16[160,1280]{1,0:T(8,128)(2,1)}, f32[160,1280]{1,0:T(8,128)}, f32[160,1280]{1,0:T(8,128)}) custom-call(s32[8]{0:T(128)} %bitcast.10, f32[8]{0:T(128)} %rates.1, s32[8]{0:T(128)} %levels.1, s16[8,10,176,128]{3,2,1,0:T(8,128)(2,1)} %get-tuple-element.10.gall, bf16[8,160,1280]{2,1,0:T(8,128)(2,1)} %get-tuple-element.11.wall, ...), custom_call_target="tpu_custom_call" | custom-call | tf_op jit(solution)/shard_map/pallas_call | solution.py:749

commit v8 on v6

--- a/solution.py
+++ b/solution.py
@@ -22,6 +22,7 @@
 PAD = 16
 CODED = ROWS + PAD
 TOP = 32000.0
+SPLIT = 3
 LAG = 2
 SCALING = 1.0 / math.sqrt(HW)
 
@@ -381,11 +382,12 @@
     late_out[pl.ds(0, 1), :] = row_one
     late_out[pl.ds(1, 1), :] = row_two
 
-    def send_late(k, _):
-        late_copy(k).start()
-        return 0
-
-    lax.fori_loop(1, ZN, send_late, 0)
+    def send_late(i, _):
+        away = (i + 1) // 2
+        late_copy(SLOTS + away * (1 - 2 * lax.rem(i, 2))).start()
+        return 0
+
+    lax.fori_loop(0, ZN - 1, send_late, 0)
     late[zz] = late_out[...]
 
     for i, (src, dst) in enumerate(state):
@@ -649,44 +651,49 @@
 ):
     p = partner[lax.axis_index("member")]
 
-    def cols(j):
-        return pl.ds(j * CB, CB)
-
-    def take(j):
-        return [
-            pltpu.make_async_copy(gall.at[p, j], gbuf.at[j], in_sem.at[0, j]),
-            pltpu.make_async_copy(mall.at[p, j], mbuf.at[j], in_sem.at[1, j]),
-            pltpu.make_async_copy(vall.at[p, j], vbuf.at[j], in_sem.at[2, j]),
-            pltpu.make_async_copy(wall.at[p, :, cols(j)], wbuf.at[j], in_sem.at[3, j]),
-        ]
-
-    def give(j):
-        return [
-            pltpu.make_async_copy(mout.at[j], new_m.at[:, cols(j)], out_sem.at[0, j]),
-            pltpu.make_async_copy(vout.at[j], new_v.at[:, cols(j)], out_sem.at[1, j]),
-            pltpu.make_async_copy(wout.at[j], new_w.at[:, cols(j)], out_sem.at[2, j]),
-        ]
-
-    for j in range(NB):
-        for copy in take(j):
+    spans = [(0, SPLIT), (SPLIT, NB)]
+
+    def take(part):
+        low, high = spans[part]
+        blocks, cols = pl.ds(low, high - low), pl.ds(low * CB, (high - low) * CB)
+        return [
+            pltpu.make_async_copy(gall.at[p, blocks], gbuf.at[blocks], in_sem.at[0, part]),
+            pltpu.make_async_copy(mall.at[p, blocks], mbuf.at[blocks], in_sem.at[1, part]),
+            pltpu.make_async_copy(vall.at[p, blocks], vbuf.at[blocks], in_sem.at[2, part]),
+            pltpu.make_async_copy(wall.at[p, :, cols], wbuf.at[:, cols], in_sem.at[3, part]),
+        ]
+
+    def give(part):
+        low, high = spans[part]
+        cols = pl.ds(low * CB, (high - low) * CB)
+        return [
+            pltpu.make_async_copy(mout.at[:, cols], new_m.at[:, cols], out_sem.at[0, part]),
+            pltpu.make_async_copy(vout.at[:, cols], new_v.at[:, cols], out_sem.at[1, part]),
+            pltpu.make_async_copy(wout.at[:, cols], new_w.at[:, cols], out_sem.at[2, part]),
+        ]
+
+    for part in (0, 1):
+        for copy in take(part):
             copy.start()
     level = jnp.full((1, CB), levels[p].astype(F32), F32)
     step_size = rates[p] * 2.0 ** ((level - 4.0) / 4.0)
-    for j in range(NB):
-        for copy in take(j):
+    for part in (0, 1):
+        for copy in take(part):
             copy.wait()
-        gradient = decode(gbuf[j])
-        first = beta_one * decode(mbuf[j]) + (1.0 - beta_one) * gradient
-        second = beta_two * decode(vbuf[j]) + (1.0 - beta_two) * gradient * gradient
-        mout[j] = first
-        vout[j] = second
-        wout[j] = (
-            wbuf[j].astype(F32) - step_size * first / (jnp.sqrt(second) + adam_eps)
-        ).astype(BF16)
-        for copy in give(j):
+        for j in range(*spans[part]):
+            cols = slice(j * CB, (j + 1) * CB)
+            gradient = decode(gbuf[j])
+            first = beta_one * decode(mbuf[j]) + (1.0 - beta_one) * gradient
+            second = beta_two * decode(vbuf[j]) + (1.0 - beta_two) * gradient * gradient
+            mout[:, cols] = first
+            vout[:, cols] = second
+            wout[:, cols] = (
+                wbuf[:, cols].astype(F32) - step_size * first / (jnp.sqrt(second) + adam_eps)
+            ).astype(BF16)
+        for copy in give(part):
             copy.start()
-    for j in range(NB):
-        for copy in give(j):
+    for part in (0, 1):
+        for copy in give(part):
             copy.wait()
 
 
@@ -705,14 +712,14 @@
         out_specs=(anywhere,) * 3,
         scratch_shapes=[
             coded,
-            pltpu.VMEM((NB, ROWS, CB), BF16),
+            pltpu.VMEM((ROWS, COLS), BF16),
             coded,
             coded,
-            pltpu.VMEM((NB, ROWS, CB), BF16),
-            pltpu.VMEM((NB, ROWS, CB), F32),
-            pltpu.VMEM((NB, ROWS, CB), F32),
-            pltpu.SemaphoreType.DMA((4, NB)),
-            pltpu.SemaphoreType.DMA((3, NB)),
+            pltpu.VMEM((ROWS, COLS), BF16),
+            pltpu.VMEM((ROWS, COLS), F32),
+            pltpu.VMEM((ROWS, COLS), F32),
+            pltpu.SemaphoreType.DMA((4, 2)),
+            pltpu.SemaphoreType.DMA((3, 2)),
         ],
         compiler_params=pltpu.CompilerParams(vmem_limit_bytes=56 * 1024 * 1024),
     )(partner, base_lr, perturb_index, gall, wall, mall, vall)

time: 122 us -> 122 us (level)
  no operation moved by 1% of the time
where the time goes in v8:
time: 122 us
  Pallas kernels  121 us (99%)
    pallas_call x1, Pallas kernels, gather_gradients(): pl.pallas_call(gradient_kernel, out_shape=(jax.ShapeDtypeStruct((MEMBERS,...  118 us
    pallas_call x1, Pallas kernels, update(): pl.pallas_call(update_kernel, out_shape=(jax.ShapeDtypeStruct((ROWS, COLS...  3.58 us

profile of v8, /device:TPU:1, one launch (start us, length us, event | category | flops | bytes accessed | tf_op | source)
XLA Modules:
  0.0 121.8 jit_solution(17102133555036800516)
XLA Ops:
  0.6 117.5 %shard_map.112 = (s16[8,5,176,256]{3,2,1,0:T(8,128)(2,1)}, bf16[8,160,1280]{2,1,0:T(8,128)(2,1)}, s16[8,5,176,256]{3,2,1,0:T(8,128)(2,1)}, s16[8,5,176,256]{3,2,1,0:T(8,128)(2,1)}) custom-call(bf16[128,1280]{1,0:T(8,128)(2,1)} %bitcast.18, bf16[160,1280]{1,0:T(8,128)(2,1)} %bitcast.16, f32[160,1280]{1,0:T(8,128)} %bitcast.12, f32[160,1280]{1,0:T(8,128)} %bitcast.13, ...), custom_call_target="tpu_custom_call" | custom-call | flops 3355443200 | bytes 20000000 | tf_op jit(solution)/shard_map/pallas_call | solution.py:585
  118.2 3.6 %shard_map.113 = (bf16[160,1280]{1,0:T(8,128)(2,1)}, f32[160,1280]{1,0:T(8,128)}, f32[160,1280]{1,0:T(8,128)}) custom-call(s32[8]{0:T(128)} %bitcast.10, f32[8]{0:T(128)} %rates.1, s32[8]{0:T(128)} %levels.1, s16[8,5,176,256]{3,2,1,0:T(8,128)(2,1)} %get-tuple-element.10.gall, bf16[8,160,1280]{2,1,0:T(8,128)(2,1)} %get-tuple-element.11.wall, ...), custom_call_target="tpu_custom_call" | custom-call | tf_op jit(solution)/shard_map/pallas_call | solution.py:704

commit v9 on v8

--- a/solution.py
+++ b/solution.py
@@ -189,6 +189,8 @@
         remote(w, wbuf.at[1, 0], in_s.at[3], in_r.at[3], dev_c),
         remote(tgt.at[:, 1 - xl], tbuf.at[1], in_s.at[4], in_r.at[4], dev_a),
     ]
+    for copy in inputs:
+        copy.start()
 
     state = [(w, wall), (mcode, mall), (vcode, vall)]
 
@@ -229,8 +231,6 @@
     swap.wait_recv()
     for d in (0, 1):
         first(1, d, xbuf.at[1, 0, 0]).start()
-    for copy in inputs:
-        copy.start()
     for copy in moments:
         copy.wait()
 

time: 122 us -> 122 us (level)
  no operation moved by 1% of the time
where the time goes in v9:
time: 122 us
  Pallas kernels  121 us (99%)
    pallas_call x1, Pallas kernels, gather_gradients(): pl.pallas_call(gradient_kernel, out_shape=(jax.ShapeDtypeStruct((MEMBERS,...  117 us
    pallas_call x1, Pallas kernels, update(): pl.pallas_call(update_kernel, out_shape=(jax.ShapeDtypeStruct((ROWS, COLS...  3.58 us

profile of v9, /device:TPU:1, one launch (start us, length us, event | category | flops | bytes accessed | tf_op | source)
XLA Modules:
  0.0 121.6 jit_solution(13840827507692419582)
XLA Ops:
  0.6 117.4 %shard_map.112 = (s16[8,5,176,256]{3,2,1,0:T(8,128)(2,1)}, bf16[8,160,1280]{2,1,0:T(8,128)(2,1)}, s16[8,5,176,256]{3,2,1,0:T(8,128)(2,1)}, s16[8,5,176,256]{3,2,1,0:T(8,128)(2,1)}) custom-call(bf16[128,1280]{1,0:T(8,128)(2,1)} %bitcast.18, bf16[160,1280]{1,0:T(8,128)(2,1)} %bitcast.16, f32[160,1280]{1,0:T(8,128)} %bitcast.12, f32[160,1280]{1,0:T(8,128)} %bitcast.13, ...), custom_call_target="tpu_custom_call" | custom-call | flops 3355443200 | bytes 20000000 | tf_op jit(solution)/shard_map/pallas_call | solution.py:585
  118.0 3.6 %shard_map.113 = (bf16[160,1280]{1,0:T(8,128)(2,1)}, f32[160,1280]{1,0:T(8,128)}, f32[160,1280]{1,0:T(8,128)}) custom-call(s32[8]{0:T(128)} %bitcast.10, f32[8]{0:T(128)} %rates.1, s32[8]{0:T(128)} %levels.1, s16[8,5,176,256]{3,2,1,0:T(8,128)(2,1)} %get-tuple-element.10.gall, bf16[8,160,1280]{2,1,0:T(8,128)(2,1)} %get-tuple-element.11.wall, ...), custom_call_target="tpu_custom_call" | custom-call | tf_op jit(solution)/shard_map/pallas_call | solution.py:704
